TPU v7x, 128 devices: a whole 4x4x4 slice. The times are simulated.
128 devices in a mesh: ctx: 32 (over z, x_hi, y), chan: 4 (over x_lo, core).
Axes of the slice: x: 4 (x_hi: 2, x_lo: 2; x = x_hi * 2 + x_lo), y: 4, z: 4, core: 2. Of those that a mesh axis runs over, the one named last changes fastest.
Arguments:
- token_ids: int32 [24576], P('ctx'), may hold values from 0 to 511
- embed_table: bfloat16 [512, 4096], P(None, 'chan'), may hold values from -6 to 6
- norm_gain: float32 [4096], replicated, may hold values from 0.1 to 1.9
- in_weight: bfloat16 [4096, 3, 2048], P('ctx', None, 'chan'), may hold values from -0.09375 to 0.09375
- short_filter: float32 [3, 3, 2048], P(None, None, 'chan'), may hold values from -3 to 3
- residue: float32 [16, 2048], P(None, 'chan'), may hold values from -1.5 to 1.5
- decay_rate: float32 [16, 2048], P(None, 'chan'), may hold values from 2.0345053e-05 to 0.033
- skip_bias: float32 [2048], P('chan'), may hold values from -4 to 4
Outputs:
- gated_output: bfloat16 [24576, 2048], P('ctx', 'chan')
All inputs are finite; a program needn't handle non-finite values.
Results may differ from a plain program's by a relative error of at most 0.014.
Values may be sent and summed in bfloat16 or wider, within the bound.
A program may use at most 128 MiB of HBM per device.

v0:
```python
import math

import jax
import jax.numpy as jnp
from jax import lax
from jax.sharding import PartitionSpec as P

norm_epsilon = 1e-06


def shifted(array, axis, by):
    devices = lax.axis_size(axis)
    pairs = [(i, i + by) for i in range(devices) if 0 <= i + by < devices]
    return lax.ppermute(array, axis, pairs)


def shortened(array):
    return jax.tree.map(lambda a: a.astype(jnp.bfloat16) if a.dtype == jnp.float32 else a, array)


def phase_table(left_index, right_index, period, direction):
    product = left_index[:, None] * right_index[None, :] % period
    angle = 2.0 * math.pi / period * product.astype(jnp.float32)
    return (jnp.cos(angle), direction * jnp.sin(angle))


def real_einsum(form, cosine, sine, signal):
    real_part = jnp.einsum(form, cosine, signal, precision=lax.Precision.HIGHEST)
    imag_part = jnp.einsum(form, sine, signal, precision=lax.Precision.HIGHEST)
    return (real_part, imag_part)


def complex_einsum(form, cosine, sine, real_in, imag_in):
    highest = lax.Precision.HIGHEST
    real_part = jnp.einsum(form, cosine, real_in, precision=highest) - jnp.einsum(
        form, sine, imag_in, precision=highest
    )
    imag_part = jnp.einsum(form, cosine, imag_in, precision=highest) + jnp.einsum(
        form, sine, real_in, precision=highest
    )
    return (real_part, imag_part)


def rotate(real_in, imag_in, cosine, sine):
    return (real_in * cosine - imag_in * sine, real_in * sine + imag_in * cosine)


def filter_spectrum(freq_index, residue_modes, decay_modes, points, seq_total):
    signed = freq_index - points * (freq_index >= points // 2).astype(jnp.int32)
    fraction = signed.astype(jnp.float32) / points
    half_sine = jnp.sin(math.pi * fraction)
    full_sine = jnp.sin(2.0 * math.pi * fraction)
    parity = 1.0 - 2.0 * (freq_index % 2).astype(jnp.float32)
    real_total = jnp.zeros_like(half_sine * residue_modes[0])
    imag_total = real_total
    for mode_index in range(residue_modes.shape[0]):
        decay_mode = decay_modes[mode_index]
        factor = jnp.exp(-decay_mode)
        weight_mode = residue_modes[mode_index] * jnp.sqrt(decay_mode)
        numerator = weight_mode * (1.0 - parity * jnp.exp(-decay_mode * seq_total))
        real_den = -jnp.expm1(-decay_mode) + 2.0 * factor * half_sine * half_sine
        imag_den = factor * full_sine
        magnitude = real_den * real_den + imag_den * imag_den
        real_total = real_total + numerator * real_den / magnitude
        imag_total = imag_total - numerator * imag_den / magnitude
    return (real_total, imag_total)


def per_device(
    token_ids, embed_table, norm_gain, in_weight, short_filter, residue, decay_rate, skip_bias
):
    seq_rows = token_ids.shape[0]
    vocab_rows = embed_table.shape[0]
    chans = short_filter.shape[2]
    onehot = (token_ids[:, None] == jnp.arange(vocab_rows, dtype=jnp.int32)[None, :]).astype(
        jnp.bfloat16
    )
    embedded_part = jnp.dot(onehot, embed_table, preferred_element_type=jnp.float32).astype(
        jnp.bfloat16
    )
    embedded = lax.all_gather(embedded_part, "chan", axis=1, tiled=True)
    wide = embedded.astype(jnp.float32)
    mean_square = jnp.mean(wide * wide, axis=-1, keepdims=True)
    normed = (wide * lax.rsqrt(mean_square + norm_epsilon) * norm_gain).astype(jnp.bfloat16)
    weight_rows = in_weight.reshape(in_weight.shape[0], 3 * chans)
    projected = jnp.dot(
        normed,
        lax.all_gather(weight_rows, "ctx", axis=0, tiled=True),
        preferred_element_type=jnp.float32,
    ).astype(jnp.bfloat16)
    taps = short_filter.shape[0]
    earlier = shifted(projected[seq_rows - (taps - 1) :], "ctx", 1)
    extended = (
        jnp.concatenate([earlier, projected], axis=0)
        .astype(jnp.float32)
        .reshape(seq_rows + taps - 1, 3, chans)
    )
    branches = jnp.zeros((seq_rows, 3, chans), jnp.float32)
    for offset in range(taps):
        begin = taps - 1 - offset
        branches = branches + short_filter[offset] * extended[begin : begin + seq_rows]
    query = branches[:, 0]
    carried = (branches[:, 1] * branches[:, 2]).astype(jnp.bfloat16)
    shards = lax.axis_size("ctx")
    index = lax.axis_index("ctx")
    doubled = 2 * shards
    span = seq_rows // shards
    seq_total = shards * seq_rows
    points = 2 * seq_total
    shard_range = jnp.arange(shards, dtype=jnp.int32)
    doubled_range = jnp.arange(doubled, dtype=jnp.int32)
    row_range = jnp.arange(seq_rows, dtype=jnp.int32)
    spread = lax.all_to_all(
        carried.reshape(1, seq_rows, chans), "ctx", split_axis=1, concat_axis=0, tiled=True
    ).astype(jnp.float32)
    cos_outer, sin_outer = phase_table(doubled_range, shard_range, doubled, -1.0)
    real_one, imag_one = real_einsum("ka,arc->krc", cos_outer, sin_outer, spread)
    rows_global = index * span + jnp.arange(span, dtype=jnp.int32)
    cos_twist, sin_twist = phase_table(doubled_range, rows_global, points, -1.0)
    real_one, imag_one = rotate(real_one, imag_one, cos_twist[:, :, None], sin_twist[:, :, None])
    moved = lax.all_to_all(
        jnp.stack([real_one, imag_one]).astype(jnp.bfloat16),
        "ctx",
        split_axis=1,
        concat_axis=2,
        tiled=True,
    ).astype(jnp.float32)
    cos_inner, sin_inner = phase_table(row_range, row_range, seq_rows, -1.0)
    real_two, imag_two = complex_einsum("kr,jrc->jkc", cos_inner, sin_inner, moved[0], moved[1])
    owned = index * 2 + jnp.arange(2, dtype=jnp.int32)
    freq_index = owned[:, None] + doubled * row_range[None, :]
    real_filter, imag_filter = filter_spectrum(
        freq_index[:, :, None], residue, decay_rate, points, float(seq_total)
    )
    real_three = real_two * real_filter - imag_two * imag_filter
    imag_three = real_two * imag_filter + imag_two * real_filter
    cos_back, sin_back = phase_table(row_range, row_range, seq_rows, 1.0)
    real_four, imag_four = complex_einsum("rk,jkc->jrc", cos_back, sin_back, real_three, imag_three)
    cos_untwist, sin_untwist = phase_table(owned, row_range, points, 1.0)
    real_four, imag_four = rotate(
        real_four, imag_four, cos_untwist[:, :, None], sin_untwist[:, :, None]
    )
    returned = lax.all_to_all(
        shortened(jnp.stack([real_four, imag_four])), "ctx", split_axis=2, concat_axis=1, tiled=True
    )
    cos_final, sin_final = phase_table(shard_range, doubled_range, doubled, 1.0)
    highest = lax.Precision.HIGHEST
    partial_conv = (
        jnp.einsum("ak,krc->arc", cos_final, returned[0], precision=highest)
        - jnp.einsum("ak,krc->arc", sin_final, returned[1], precision=highest)
    ) / points
    long_conv = (
        lax.all_to_all(shortened(partial_conv), "ctx", split_axis=0, concat_axis=1, tiled=True)
        .astype(partial_conv.dtype)
        .reshape(seq_rows, chans)
    )
    gated_output = query * (long_conv + skip_bias * carried.astype(jnp.float32))
    return gated_output.astype(jnp.bfloat16)


def solution(mesh):
    return jax.shard_map(
        per_device,
        mesh=mesh,
        in_specs=(
            P("ctx"),
            P(None, "chan"),
            P(),
            P("ctx", None, "chan"),
            P(None, None, "chan"),
            P(None, "chan"),
            P(None, "chan"),
            P("chan"),
        ),
        out_specs=P("ctx", "chan"),
        check_vma=False,
    )
```

profile of v0, /device:TPU:0, one launch (start us, length us, event | category | flops | bytes accessed | tf_op | source)
XLA Modules:
  0.0 654.3 jit_solution(11139075171301220877)
XLA Ops:
  11.7 64.7 %all-gather.3.cloned.1.call-done = bf16[768,4096]{1,0:T(8,128)(2,1)} async-done(((bf16[768,1024]{1,0:T(8,128)(2,1)}), bf16[768,4096]{1,0:T(8,128)(2,1)}) %all-gather.3.cloned.1.call-update) | async-done | bytes 6291472 | tf_op jit(solution)/shard_map/all_gather | solution.py:81
  80.4 170.0 %all-gather.5.cloned.1.call-done = bf16[4096,1536]{0,1:T(8,128)(2,1)} async-done(((bf16[128,1536]{0,1:T(8,128)(2,1)}), bf16[4096,1536]{0,1:T(8,128)(2,1)}) %all-gather.5.cloned.1.call-update) | async-done | bytes 12582928 | tf_op jit(solution)/shard_map/all_gather | solution.py:88
  250.4 14.8 %fusion.7 = bf16[768,1536]{1,0:T(8,128)(2,1)S(1)} fusion(bf16[4096,1536]{0,1:T(8,128)(2,1)} %all-gather.5.cloned.1.call-done, bf16[768,4096]{1,0:T(8,128)(2,1)} %all-gather.3.cloned.1.call-done, f32[4096]{0:T(1024)S(1)} %copy-done.12, f32[768]{0:T(1024)S(1)} %add_rsqrt_fusion), kind=kOutput, calls=%fused_computation.42 | convolution fusion | flops 9677438976 | bytes 21253120 | tf_op jit(solution)/shard_map/dot_general | solution.py:86
  272.8 10.5 %fusion.246 = (f32[768,1536]{1,0:T(8,128)}, f32[768,1536]{1,0:T(8,128)}, f32[768,1536]{1,0:T(8,128)}) fusion(f32[770,1536]{1,0:T(8,128)} %maximum_convert_fusion), kind=kLoop, calls=%fused_computation.407 | loop fusion | bytes 28311552 | tf_op jit(solution)/shard_map/slice | solution.py:101
  283.3 6.0 copy.54
  289.4 6.1 copy.56
  295.5 6.1 copy.55
  301.5 5.6 multiply_add_fusion
  311.3 5.4 reduce
  317.9 8.7 %all-to-all-start = ((bf16[32,2,6144]{2,1,0:T(2,128)(2,1)}), bf16[32,2,6144]{2,1,0:T(2,128)(2,1)S(1)}, u32[]{:S(2)}, u32[]{:S(2)}) async-start(bf16[32,2,6144]{2,1,0:T(2,128)(2,1)} %reshape.926), calls=%async_computation | async-start | bytes 1572864 | tf_op jit(solution)/shard_map/all_to_all | solution.py:113
  326.6 10.0 %fusion.97.clone.4 = f32[768,768,1]{1,0,2:T(8,128)} fusion(), kind=kLoop, calls=%fused_computation.144.clone.clone.clone.clone.clone.1 | loop fusion | flops 5898240 | bytes 2359296 | tf_op jit(solution)/shard_map/add | solution.py:136
  349.4 7.0 %all-to-all-start.1 = ((bf16[2,64,24,512]{3,2,0,1:T(8,128)(2,1)}), bf16[2,64,24,512]{3,2,0,1:T(8,128)(2,1)}, u32[]{:S(2)}, u32[]{:S(2)}) async-start(bf16[2,64,24,512]{3,2,0,1:T(8,128)(2,1)} %copy.60), calls=%async_computation.1 | async-start | bytes 6291456 | tf_op jit(solution)/shard_map/all_to_all | solution.py:121
  357.6 37.1 %all-to-all-done.1 = bf16[2,64,24,512]{3,2,0,1:T(8,128)(2,1)} async-done(((bf16[2,64,24,512]{3,2,0,1:T(8,128)(2,1)}), bf16[2,64,24,512]{3,2,0,1:T(8,128)(2,1)}, u32[]{:S(2)}, u32[]{:S(2)}) %all-to-all-start.1) | async-done | bytes 3145760 | tf_op jit(solution)/shard_map/all_to_all | solution.py:121
  397.4 14.6 %fusion.74 = f32[2,512,768]{2,1,0:T(8,128)S(1)} fusion(bf16[2,768,512]{2,1,0:T(8,128)(2,1)S(1)} %bitcast.204), kind=kOutput, calls=%fused_computation.151 | convolution fusion | flops 7253065728 | bytes 4718592 | tf_op jit(solution)/shard_map/kr,jrc->jkc/dot_general | solution.py:38
  412.0 14.7 %fusion.76 = f32[2,512,768]{2,1,0:T(8,128)S(1)} fusion(bf16[2,768,512]{2,1,0:T(8,128)(2,1)S(1)} %bitcast.202), kind=kOutput, calls=%fused_computation.153 | convolution fusion | flops 7253065728 | bytes 4718592 | tf_op jit(solution)/shard_map/kr,jrc->jkc/dot_general | solution.py:35
  426.8 15.0 %fusion.92 = f32[2,512,768]{2,1,0:T(8,128)S(1)} fusion(f32[2,512,768]{2,1,0:T(8,128)S(1)} %fusion.76, bf16[2,768,512]{2,1,0:T(8,128)(2,1)S(1)} %bitcast.205), kind=kOutput, calls=%fused_computation.162 | convolution fusion | flops 7254441984 | bytes 7864320 | tf_op jit(solution)/shard_map/kr,jrc->jkc/dot_general | solution.py:35
  441.7 34.6 %fusion.59 = (f32[2,768,512]{1,2,0:T(8,128)S(1)}, f32[2,768,512]{1,2,0:T(8,128)S(1)}, f32[2,768,512]{1,2,0:T(8,128)S(1)}, f32[2,512,768]{2,1,0:T(8,128)S(1)}) fusion(f32[2,512,768]{2,1,0:T(8,128)S(1)} %fusion.92, f32[512]{0:T(512)S(1)} %bitcast.208, f32[512]{0:T(512)S(1)} %get-tuple-element.97, f32[512]{0:T(512)S(1)} %bitcast.286, f32[512]{0:T(512)S(1)} %bitcast.264, ...), kind=kOutput, calls=%fused_computation.96 | convolution fusion | flops 7451443200 | bytes 22988800 | tf_op jit(solution)/shard_map/kr,jrc->jkc/dot_general | solution.py:38
  477.1 18.3 %fusion.62 = f32[2,512,768]{2,1,0:T(8,128)S(1)} fusion(f32[2,768,512]{1,2,0:T(8,128)S(1)} %fusion.58), kind=kOutput, calls=%fused_computation.139 | convolution fusion | flops 7253065728 | bytes 6291456 | tf_op jit(solution)/shard_map/rk,jkc->jrc/dot_general | solution.py:38
  495.4 17.9 %fusion.64 = f32[2,512,768]{2,1,0:T(8,128)S(1)} fusion(f32[2,768,512]{1,2,0:T(8,128)S(1)} %get-tuple-element.5), kind=kOutput, calls=%fused_computation.141 | convolution fusion | flops 7253065728 | bytes 6291456 | tf_op jit(solution)/shard_map/rk,jkc->jrc/dot_general | solution.py:35
  513.4 18.1 %fusion.98 = f32[2,512,768]{2,1,0:T(8,128)S(1)} fusion(f32[2,512,768]{2,1,0:T(8,128)S(1)} %fusion.64, f32[2,768,512]{1,2,0:T(8,128)S(1)} %fusion.58), kind=kOutput, calls=%fused_computation.164 | convolution fusion | flops 7253852160 | bytes 9437184 | tf_op jit(solution)/shard_map/rk,jkc->jrc/dot_general | solution.py:35
  531.5 17.3 %fusion.106 = (bf16[1,2,768,512]{2,3,1,0:T(8,128)(2,1)S(1)}, bf16[1,2,768,512]{2,3,1,0:T(8,128)(2,1)S(1)}) fusion(f32[2,512,768]{2,1,0:T(8,128)S(1)} %fusion.98, f32[2,768]{1,0:T(2,128)S(1)} %copy-done.10, f32[2,768]{1,0:T(2,128)S(1)} %copy-done.9, f32[2,512,768]{2,1,0:T(8,128)S(1)} %fusion.62, f32[2,768,512]{1,2,0:T(8,128)S(1)} %get-tuple-element.5), kind=kOutput, calls=%fused_computation.169 | convolution fusion | flops 7260143616 | bytes 12595200 | tf_op jit(solution)/shard_map/rk,jkc->jrc/dot_general | solution.py:38
  550.7 8.7 %copy.68 = bf16[2,2,768,512]{3,1,0,2:T(2,128)(2,1)} copy(bf16[2,2,768,512]{2,3,1,0:T(8,128)(2,1)} %pad_maximum_fusion.1) | data formatting | bytes 6291456 | tf_op jit(solution)/shard_map/stack | solution.py:144
  559.4 47.3 %all_to_all.51 = bf16[2,2,768,512]{3,1,0,2:T(2,128)(2,1)S(1)} all-to-all(bf16[2,2,768,512]{3,1,0,2:T(2,128)(2,1)} %copy.68), channel_id=1, replica_groups=mesh['ctx'=32,'chan'=4] {'ctx'}, dimensions={2} | all-to-all | bytes 6291456 | tf_op jit(solution)/shard_map/all_to_all | solution.py:143
  621.3 19.7 %all_to_all.52 = bf16[32,24,512]{2,1,0:T(8,128)(2,1)S(1)} all-to-all(bf16[32,24,512]{2,1,0:T(8,128)(2,1)S(1)} %copy.72), channel_id=1, replica_groups=mesh['ctx'=32,'chan'=4] {'ctx'}, dimensions={0} | all-to-all | bytes 1572864 | tf_op jit(solution)/shard_map/all_to_all | solution.py:153
  (87 shorter events, 61.9 us)
Async XLA Ops:
  6.5 1.2 copy-start
  6.5 4.2 copy-start.5
  6.5 69.8 %all-gather.3.cloned.1.call-start = ((), (), s32[]{:S(2)}) async-start(), calls=%async_computation.4 | async-start | bytes 7864320 | tf_op jit(solution)/shard_map/all_gather | solution.py:81
  10.6 239.8 %all-gather.5.cloned.1.call-start = ((), (), s32[]{:S(2)}) async-start(), calls=%async_computation.5 | async-start | bytes 12976128 | tf_op jit(solution)/shard_map/all_gather | solution.py:88
  11.6 238.8 %copy-start.12 = (f32[4096]{0:T(1024)S(1)}, f32[4096]{0:T(1024)}, u32[]{:S(2)}) copy-start(f32[4096]{0:T(1024)} %param.10) | copy-start | bytes 49156
  80.4 188.4 %copy-start.8 = (f32[3,3,512]{2,1,0:T(4,128)S(1)}, f32[3,3,512]{2,1,0:T(4,128)}, u32[]{:S(2)}) copy-start(f32[3,3,512]{2,1,0:T(4,128)} %param.12) | copy-start | bytes 55300
  265.3 4.7 collective-permute-start
  307.2 2.1 copy-start.2
  316.7 20.0 %copy-start.6 = (f32[16,512]{1,0:T(8,128)S(1)}, f32[16,512]{1,0:T(8,128)}, u32[]{:S(2)}) copy-start(f32[16,512]{1,0:T(8,128)} %param.14) | copy-start | bytes 98308
  317.9 22.5 %all-to-all-start = ((bf16[32,2,6144]{2,1,0:T(2,128)(2,1)}), bf16[32,2,6144]{2,1,0:T(2,128)(2,1)S(1)}, u32[]{:S(2)}, u32[]{:S(2)}) async-start(bf16[32,2,6144]{2,1,0:T(2,128)(2,1)} %reshape.926), calls=%async_computation | async-start | bytes 1572864 | tf_op jit(solution)/shard_map/all_to_all | solution.py:113
  349.3 8.2 %copy-start.7 = (f32[16,512]{1,0:T(8,128)S(1)}, f32[16,512]{1,0:T(8,128)}, u32[]{:S(2)}) copy-start(f32[16,512]{1,0:T(8,128)} %param.13) | copy-start | bytes 98308
  349.4 45.4 %all-to-all-start.1 = ((bf16[2,64,24,512]{3,2,0,1:T(8,128)(2,1)}), bf16[2,64,24,512]{3,2,0,1:T(8,128)(2,1)}, u32[]{:S(2)}, u32[]{:S(2)}) async-start(bf16[2,64,24,512]{3,2,0,1:T(8,128)(2,1)} %copy.60), calls=%async_computation.1 | async-start | bytes 6291456 | tf_op jit(solution)/shard_map/all_to_all | solution.py:121
  426.8 15.0 %copy-start.4 = (f32[768,768,1]{1,0,2:T(8,128)S(1)}, f32[768,768,1]{1,0,2:T(8,128)}, u32[]{:S(2)}) copy-start(f32[768,768,1]{1,0,2:T(8,128)} %fusion.97.clone.4) | copy-start | bytes 7077892
  513.4 18.1 %copy-start.9 = (f32[2,768]{1,0:T(2,128)S(1)}, f32[2,768]{1,0:T(2,128)}, u32[]{:S(2)}) copy-start(f32[2,768]{1,0:T(2,128)} %get-tuple-element.89) | copy-start | bytes 18436
  513.4 18.1 %copy-start.10 = (f32[2,768]{1,0:T(2,128)S(1)}, f32[2,768]{1,0:T(2,128)}, u32[]{:S(2)}) copy-start(f32[2,768]{1,0:T(2,128)} %get-tuple-element.90) | copy-start | bytes 18436
  617.5 2.4 copy-start.3
  641.0 2.0 copy-start.11
  641.2 6.0 copy-start.1
Sparse Core Ops, SparseCore 0:
  10.8 65.5 all-gather.2
  79.1 171.3 all-gather.4
where the time goes:
time: 660 us; the launch traced here: 654 us
  waiting for transfers between devices  277 us (42%)
  matrix products  176 us (27%)
  blocking collectives  67 us (10%)
  local copies, waits for them, and re-layouts  65.8 us (10%)
  other arithmetic  35.9 us (5%)
  starting transfers between devices  19.3 us (3%)
  between operations  14.2 us (2%)
    all_gather x1, waiting for transfers between devices, per_device(): lax.all_gather(weight_rows, 'ctx', axis=0, tiled=True)  170 us
    all_gather x1, waiting for transfers between devices, per_device(): embedded = lax.all_gather(embedded_part, 'chan', axis=1, tiled=True)  64.7 us
    dot_general x2, matrix products, complex_einsum(): jnp.einsum(form, sine, real_in, precision=highest)  52.9 us
    all_to_all x1, blocking collectives, per_device(): lax.all_to_all(shortened(jnp.stack([real_four, imag_four])), 'ctx', split...  47.3 us
    all_to_all x1, waiting for transfers between devices, per_device(): lax.all_to_all(jnp.stack([real_one, imag_one]).astype(jnp.bfloat16), 'ctx...  37.1 us
    dot_general x2, matrix products, complex_einsum(): jnp.einsum(form, sine, imag_in, precision=highest)  32.9 us
    dot_general x2, matrix products, complex_einsum(): jnp.einsum(form, cosine, real_in, precision=highest)  32.8 us
    dot_general x2, matrix products, complex_einsum(): jnp.einsum(form, cosine, imag_in, precision=highest)  31.9 us
  transfers between devices with their start and end apart: 5, of which 5 were waited for; matrix products, arithmetic and copies ran while one was open for 3% of the time, Pallas kernels for 0%

commit v1 on v0

v1 whole, which is shorter than its diff:
```python
import functools

import jax
import jax.numpy as jnp
from jax import lax
from jax.experimental import pallas as pl
from jax.experimental.pallas import tpu as pltpu
from jax.sharding import PartitionSpec as P

MESH = pl.DeviceIdType.MESH
EPS = 1e-06
VMEM_LIMIT = 48 * 1024 * 1024

CTX, CHAN, PLANE = 32, 4, 8
OWN = 16
SEG = 256
SEGS = 96
PER = 3
MODES = 16
NT = (((1,), (1,)), ((), ()))
HIGHEST = lax.Precision.HIGHEST


def dot(a, b):
    return jnp.dot(a, b, preferred_element_type=jnp.float32)


def high_low(x):
    high = x.astype(jnp.bfloat16)
    return high, (x - high.astype(jnp.float32)).astype(jnp.bfloat16)


def send(src, dst, send_sem, recv_sem, i, c):
    return pltpu.make_async_remote_copy(
        src_ref=src, dst_ref=dst, send_sem=send_sem, recv_sem=recv_sem, device_id=(i, c), device_id_type=MESH
    )


def table_kernel(
    tok_ref, embed_ref, gain_ref, weight_ref, table_ref, tokens_ref,
    got_weight, got_square, part, part_send, part_got, scaled,
    w_send, w_recv, t_send, t_recv, s_send, s_recv, p_send, p_recv,
):
    i, c = lax.axis_index("ctx"), lax.axis_index("chan")
    plane, place = i // PLANE, i % PLANE

    barrier = pltpu.get_barrier_semaphore()

    @pl.loop(0, CTX)
    def _(j):
        row, col = c * PLANE + j % PLANE, j // PLANE

        @pl.when(jnp.logical_or(row != i, col != c))
        def _():
            pl.semaphore_signal(barrier, inc=1, device_id=(row, col), device_id_type=MESH)

    @pl.loop(1, CTX)
    def _(j):
        pl.semaphore_signal(barrier, inc=1, device_id=((i + j) % CTX, c), device_id_type=MESH)

    for d in range(1, CHAN):
        pl.semaphore_signal(barrier, inc=1, device_id=(i, (c + d) % CHAN), device_id_type=MESH)
    own = jnp.where(plane == c, 1, 0)
    pl.semaphore_wait(barrier, CTX - own + (CTX - 1) + (CHAN - 1))

    def weight_copy(j):
        to = (i + j) % CTX
        return send(
            weight_ref.at[:, pl.ds(to * OWN, OWN), :],
            got_weight.at[c, :, :, pl.ds(place * 128, 128)],
            w_send.at[j],
            w_recv.at[c * PLANE + place],
            to,
            plane,
        )

    def token_copy(j):
        return send(tok_ref, tokens_ref.at[i], t_send.at[j], t_recv.at[i], (i + j) % CTX, c)

    @pl.loop(1, CTX)
    def _(j):
        weight_copy(j).start()

    self_copy = pltpu.make_async_copy(
        weight_ref.at[:, pl.ds(i * OWN, OWN), :],
        got_weight.at[c, :, :, pl.ds(place * 128, 128)],
        w_recv.at[c * PLANE + place],
    )

    @pl.when(plane == c)
    def _():
        self_copy.start()

    @pl.when(plane != c)
    def _():
        weight_copy(0).start()

    own_tokens = pltpu.make_async_copy(tok_ref, tokens_ref.at[i], t_recv.at[i])
    own_tokens.start()

    @pl.loop(1, CTX)
    def _(j):
        token_copy(j).start()

    wide = embed_ref[...].astype(jnp.float32)
    square_high, square_low = high_low(wide * wide)
    ones = jnp.ones((8, square_high.shape[1]), jnp.bfloat16)
    squares = lax.dot_general(ones, square_high, NT, preferred_element_type=jnp.float32)
    squares = squares + lax.dot_general(ones, square_low, NT, preferred_element_type=jnp.float32)
    got_square[c] = squares
    scaled[...] = (wide * gain_ref[c]).astype(jnp.bfloat16)

    def square_copy(d):
        return send(got_square.at[c], got_square.at[c], s_send.at[d], s_recv.at[c], i, (c + d) % CHAN)

    for d in range(1, CHAN):
        square_copy(d).start()

    @pl.loop(0, CTX)
    def _(s):
        pltpu.make_async_copy(
            weight_ref.at[:, pl.ds(0, OWN), :],
            got_weight.at[s // PLANE, :, :, pl.ds((s % PLANE) * 128, 128)],
            w_recv.at[s],
        ).wait()

    def part_copy(d):
        to = (c + d) % CHAN
        return send(part_send.at[to], part_got.at[c], p_send.at[d], p_recv.at[c], i, to)

    for q in range(CHAN):
        weights = got_weight[q].reshape(3 * OWN, got_weight.shape[3])
        product = lax.dot_general(weights, scaled[...], NT, preferred_element_type=jnp.float32)
        part[q] = product
        part_send[q] = product.astype(jnp.bfloat16)
    for d in range(1, CHAN):
        part_copy(d).start()
    total = part[c]
    mean = got_square[c]
    for d in range(1, CHAN):
        source = (c + d) % CHAN
        send(got_square.at[c], got_square.at[source], s_send.at[d], s_recv.at[source], i, source).wait_recv()
        mean = mean + got_square[source]
    scale = lax.rsqrt(mean[0:1] * (1.0 / (CHAN * embed_ref.shape[1])) + EPS)
    for d in range(1, CHAN):
        source = (c + d) % CHAN
        send(part_send.at[0], part_got.at[source], p_send.at[d], p_recv.at[source], i, source).wait_recv()
        total = total + part_got[source].astype(jnp.float32)
    table_ref[...] = (total * scale).astype(jnp.bfloat16)

    @pl.loop(0, CTX)
    def _(s):
        pltpu.make_async_copy(tok_ref, tokens_ref.at[s], t_recv.at[s]).wait()

    @pl.loop(1, CTX)
    def _(j):
        weight_copy(j).wait_send()
        token_copy(j).wait_send()

    @pl.when(plane != c)
    def _():
        weight_copy(0).wait_send()

    for d in range(1, CHAN):
        square_copy(d).wait_send()
        part_copy(d).wait_send()


def table_and_tokens(token_ids, embed_table, norm_gain, in_weight):
    rows = token_ids.shape[0]
    vocab, feats = embed_table.shape
    weight = jnp.transpose(in_weight, (1, 2, 0))
    dma = pltpu.SemaphoreType.DMA
    return pl.pallas_call(
        table_kernel,
        name="table",
        out_shape=(
            jax.ShapeDtypeStruct((3 * OWN, vocab), jnp.bfloat16),
            jax.ShapeDtypeStruct((CTX, 1, rows), jnp.int32),
        ),
        in_specs=[pl.BlockSpec(memory_space=pltpu.VMEM)] * 4,
        out_specs=(pl.BlockSpec(memory_space=pltpu.VMEM),) * 2,
        scratch_shapes=[
            pltpu.VMEM((CHAN, 3, OWN, feats), jnp.bfloat16),
            pltpu.VMEM((CHAN, 8, vocab), jnp.float32),
            pltpu.VMEM((CHAN, 3 * OWN, vocab), jnp.float32),
            pltpu.VMEM((CHAN, 3 * OWN, vocab), jnp.bfloat16),
            pltpu.VMEM((CHAN, 3 * OWN, vocab), jnp.bfloat16),
            pltpu.VMEM((vocab, feats), jnp.bfloat16),
            dma((CTX,)), dma((CTX,)), dma((CTX,)), dma((CTX,)),
            dma((CHAN,)), dma((CHAN,)), dma((CHAN,)), dma((CHAN,)),
        ],
        compiler_params=pltpu.CompilerParams(
            collective_id=0, has_side_effects=True, vmem_limit_bytes=VMEM_LIMIT
        ),
    )(token_ids.reshape(1, rows), embed_table, norm_gain.reshape(CHAN, 1, feats), weight)


def conv_kernel(
    table_ref, tokens_ref, taps_ref, residue_ref, decay_ref, skip_ref, out_ref,
    toeplitz, carried_ref, query_ref, result,
):
    first = lax.axis_index("ctx") * OWN
    chans = decay_ref.shape[1]
    f32, bf16 = jnp.float32, jnp.bfloat16

    chosen = lax.broadcasted_iota(jnp.int32, (OWN, chans), 1) == first + lax.broadcasted_iota(
        jnp.int32, (OWN, chans), 0
    )

    def column(row):
        return jnp.sum(jnp.where(chosen, row, 0.0), axis=1, keepdims=True)

    decay_all = decay_ref[...]
    weight_all = residue_ref[...] * jnp.sqrt(decay_all)
    lane = lax.broadcasted_iota(jnp.int32, (OWN, SEG), 1)
    steps = lane.astype(f32)
    taps_long = jnp.zeros((OWN, SEG), f32)
    for m in range(MODES):
        taps_long = taps_long + column(weight_all[m : m + 1]) * jnp.exp(-column(decay_all[m : m + 1]) * steps)
    square_row = lax.broadcasted_iota(jnp.int32, (SEG, SEG), 0)
    square_lane = lax.broadcasted_iota(jnp.int32, (SEG, SEG), 1)
    causal = square_lane >= square_row
    for ch in range(OWN):
        spread = jnp.broadcast_to(taps_long[ch : ch + 1], (SEG, SEG))
        rolled = pltpu.roll(spread, 0, axis=1, stride=1, stride_axis=0)
        toeplitz[ch] = jnp.where(causal, rolled, 0.0).astype(bf16)

    pairs = OWN * MODES
    row_of = lax.broadcasted_iota(jnp.int32, (chans, pairs), 0)
    pick = (row_of == first + lax.broadcasted_iota(jnp.int32, (chans, pairs), 1) // MODES).astype(f32)
    own_mode = (
        lax.broadcasted_iota(jnp.int32, (MODES, pairs), 0)
        == lax.broadcasted_iota(jnp.int32, (MODES, pairs), 1) % MODES
    )

    def pair_row(array):
        wide = jnp.dot(array, pick, precision=HIGHEST, preferred_element_type=f32)
        return jnp.sum(jnp.where(own_mode, wide, 0.0), axis=0, keepdims=True)

    decay_row = pair_row(decay_all)
    decay_col = jnp.transpose(jnp.broadcast_to(decay_row, (128, pairs)))[:, 0:1]
    weight_col = jnp.transpose(jnp.broadcast_to(pair_row(weight_all), (128, pairs)))[:, 0:1]
    to_end = (SEG - 1 - square_row).astype(f32)
    gather_high, gather_low = high_low(jnp.exp(-decay_row * to_end))
    spread_high, spread_low = high_low(weight_col * jnp.exp(-decay_col * (square_lane + 1).astype(f32)))

    table = jnp.concatenate([table_ref[:, :SEG], table_ref[:, SEG:]], axis=0)
    taps = []
    for j in range(3):
        taps.append(
            jnp.concatenate([column(taps_ref[j, b : b + 1, :]) for b in range(3)], axis=0)
        )
    vocab_row = lax.broadcasted_iota(jnp.int32, (SEG, SEG), 0)

    def segment(g, part, before):
        ids = tokens_ref[g, :, part * SEG : (part + 1) * SEG]
        onehot = jnp.where(vocab_row == (ids & (SEG - 1)), 1.0, 0.0).astype(bf16)
        both = dot(table, onehot)
        projected = jnp.where(ids >= SEG, both[3 * OWN :], both[: 3 * OWN])
        longer = jnp.concatenate([before, projected], axis=1)
        branches = (
            taps[0] * projected
            + taps[1] * pltpu.roll(longer, 1, axis=1)[:, 128:]
            + taps[2] * pltpu.roll(longer, 2, axis=1)[:, 128:]
        )
        carried = (branches[OWN : 2 * OWN] * branches[2 * OWN :]).astype(bf16).astype(f32)
        at = pl.ds(g * PER + part, OWN, stride=SEGS)
        for half in range(2):
            carried_ref[half, at, :] = carried[:, half * 128 : (half + 1) * 128]
            query_ref[half, at, :] = branches[:OWN, half * 128 : (half + 1) * 128]
        return projected[:, SEG - 128 :]

    def block(g, before):
        for part in range(PER):
            before = segment(g, part, before)
        return before

    lax.fori_loop(0, SEGS // PER, block, jnp.zeros((3 * OWN, 128), f32), unroll=2)

    def both_halves(ref, ch):
        return jnp.concatenate([ref[half, ch * SEGS : (ch + 1) * SEGS, :] for half in range(2)], axis=1)

    channel_of = lax.broadcasted_iota(jnp.int32, (SEGS, pairs), 1) // MODES
    added = jnp.zeros((SEGS, pairs), f32)
    for ch in range(OWN):
        signal = both_halves(carried_ref, ch).astype(bf16)
        added = added + jnp.where(channel_of == ch, dot(signal, gather_high) + dot(signal, gather_low), 0.0)

    def later(x, by):
        return jnp.concatenate([jnp.zeros((by, pairs), f32), x[: SEGS - by]], axis=0)

    state = later(added, 1)
    by = 1
    while by < SEGS:
        state = state + jnp.exp(-decay_row * float(SEG * by)) * later(state, by)
        by *= 2
    state_high, state_low = high_low(state)

    zero = jnp.zeros((), bf16)
    skip_column = column(skip_ref[...])
    for ch in range(OWN):
        carried = both_halves(carried_ref, ch)
        high = jnp.where(channel_of == ch, state_high, zero)
        low = jnp.where(channel_of == ch, state_low, zero)
        conv = dot(carried.astype(bf16), toeplitz[ch])
        conv = conv + dot(high, spread_high) + dot(low, spread_high) + dot(high, spread_low)
        gated = both_halves(query_ref, ch) * (conv + skip_column[ch : ch + 1] * carried)
        for half in range(2):
            result[half, pl.ds(ch, SEGS, stride=OWN), :] = gated[:, half * 128 : (half + 1) * 128]
    out_ref[...] = jnp.concatenate([result[half] for half in range(2)], axis=1).astype(bf16)


def convolved(table, tokens, short_filter, residue, decay_rate, skip_bias):
    f32 = jnp.float32
    return pl.pallas_call(
        conv_kernel,
        name="conv",
        out_shape=jax.ShapeDtypeStruct((SEGS * OWN, SEG), jnp.bfloat16),
        in_specs=[pl.BlockSpec(memory_space=pltpu.VMEM)] * 6,
        out_specs=pl.BlockSpec(memory_space=pltpu.VMEM),
        scratch_shapes=[
            pltpu.VMEM((OWN, SEG, SEG), jnp.bfloat16),
            pltpu.VMEM((2, OWN * SEGS, 128), f32),
            pltpu.VMEM((2, OWN * SEGS, 128), f32),
            pltpu.VMEM((2, SEGS * OWN, 128), f32),
        ],
        compiler_params=pltpu.CompilerParams(vmem_limit_bytes=VMEM_LIMIT),
    )(table, tokens, short_filter, residue, decay_rate, skip_bias.reshape(1, -1))


def exchange_kernel(out_ref, got_ref, send_sem, recv_sem):
    i, c = lax.axis_index("ctx"), lax.axis_index("chan")
    barrier = pltpu.get_barrier_semaphore()

    @pl.loop(1, CTX)
    def _(j):
        pl.semaphore_signal(barrier, inc=1, device_id=((i + j) % CTX, c), device_id_type=MESH)

    pl.semaphore_wait(barrier, CTX - 1)

    def copy(j):
        to = (i + j) % CTX
        return send(
            out_ref.at[to], got_ref.at[:, pl.ds(i * OWN, OWN), :], send_sem.at[j], recv_sem.at[i], to, c
        )

    @pl.loop(1, CTX)
    def _(j):
        copy(j).start()

    own = pltpu.make_async_copy(out_ref.at[i], got_ref.at[:, pl.ds(i * OWN, OWN), :], recv_sem.at[i])
    own.start()

    @pl.loop(0, CTX)
    def _(s):
        pltpu.make_async_copy(out_ref.at[0], got_ref.at[:, pl.ds(s * OWN, OWN), :], recv_sem.at[s]).wait()

    @pl.loop(1, CTX)
    def _(j):
        copy(j).wait_send()


def exchanged(out):
    dma = pltpu.SemaphoreType.DMA
    return pl.pallas_call(
        exchange_kernel,
        name="exchange",
        out_shape=jax.ShapeDtypeStruct((PER, CTX * OWN, SEG), jnp.bfloat16),
        in_specs=[pl.BlockSpec(memory_space=pltpu.VMEM)],
        out_specs=pl.BlockSpec(memory_space=pltpu.VMEM),
        scratch_shapes=[dma((CTX,)), dma((CTX,))],
        compiler_params=pltpu.CompilerParams(
            collective_id=1, has_side_effects=True, vmem_limit_bytes=VMEM_LIMIT
        ),
    )(out.reshape(CTX, PER, OWN, SEG))


def turn_kernel(got_ref, out_ref):
    unit = (
        lax.broadcasted_iota(jnp.int32, (SEG, SEG), 0) == lax.broadcasted_iota(jnp.int32, (SEG, SEG), 1)
    ).astype(jnp.bfloat16)
    for g in range(PER):
        turned = lax.dot_general(unit, got_ref[g], NT, preferred_element_type=jnp.float32)
        out_ref[g * SEG : (g + 1) * SEG, :] = turned.astype(jnp.bfloat16)


def turned(got):
    return pl.pallas_call(
        turn_kernel,
        name="turn",
        out_shape=jax.ShapeDtypeStruct((PER * SEG, got.shape[1]), jnp.bfloat16),
        in_specs=[pl.BlockSpec(memory_space=pltpu.VMEM)],
        out_specs=pl.BlockSpec(memory_space=pltpu.VMEM),
        compiler_params=pltpu.CompilerParams(vmem_limit_bytes=VMEM_LIMIT),
    )(got)


def per_device(
    token_ids, embed_table, norm_gain, in_weight, short_filter, residue, decay_rate, skip_bias
):
    table, tokens = table_and_tokens(token_ids, embed_table, norm_gain, in_weight)
    out = convolved(table, tokens, short_filter, residue, decay_rate, skip_bias)
    return turned(exchanged(out))


def solution(mesh):
    return jax.shard_map(
        per_device,
        mesh=mesh,
        in_specs=(
            P("ctx"),
            P(None, "chan"),
            P(),
            P("ctx", None, "chan"),
            P(None, None, "chan"),
            P(None, "chan"),
            P(None, "chan"),
            P("chan"),
        ),
        out_specs=P("ctx", "chan"),
        check_vma=False,
    )
```

time: 660 us -> 64.1 us (0.10)
  waiting for transfers between devices: 277 us -> 0 us
  matrix products: 176 us -> 0 us
  blocking collectives: 67 us -> 0 us
  local copies, waits for them, and re-layouts: 65.8 us -> 3.8 us
  Pallas kernels: 0 us -> 59.3 us
  other arithmetic: 35.9 us -> 0 us
  starting transfers between devices: 19.3 us -> 0 us
  between operations: 14.2 us -> 0.08 us
    all_gather x2 -> x0, waiting for transfers between devices: 235 us -> none  [the longest x1 170 us: per_device(): lax.all_gather(weight_rows, 'ctx', axis=0, tiled=True)]
    dot_general x14 -> x0, matrix products: 176 us -> none  [the longest x2 52.9 us: complex_einsum(): jnp.einsum(form, sine, real_in, precision=highest)]
    all_to_all x2 -> x0, blocking collectives: 67 us -> none  [the longest x1 47.3 us: per_device(): lax.all_to_all(shortened(jnp.stack([real_four, imag_four])), 'ctx', split...]
    pallas_call x0 -> x4, Pallas kernels: none -> 59.3 us  [the longest x1 26.8 us: table_and_tokens(): pl.pallas_call(table_kernel, name='table', out_shape=(jax.ShapeDtypeStruc...]
    all_to_all x2 -> x0, waiting for transfers between devices: 40.8 us -> none  [the longest x1 37.1 us: per_device(): lax.all_to_all(jnp.stack([real_one, imag_one]).astype(jnp.bfloat16), 'ctx...]
    slice x11 -> x0, local copies, waits for them, and re-layouts: 35.2 us -> none  [the longest x4 28.7 us: per_device(): extended[begin:begin + seq_rows]]
    all_to_all x2 -> x0, starting transfers between devices: 15.7 us -> none  [the longest x1 8.69 us: per_device(): lax.all_to_all(carried.reshape(1, seq_rows, chans), 'ctx', split_axis=1,...]
    add x4 -> x0, other arithmetic: 15.6 us -> none  [the longest x1 9.96 us: per_device(): imag_three = real_two * imag_filter + imag_two * real_filter]
  transfers between devices with their start and end apart: 5 -> 0, of which waited for: 5 -> 0; matrix products, arithmetic and copies ran while one was open for 3% -> 0% of each run, Pallas kernels for 0% -> 0%
where the time goes in v1:
time: 64.1 us; the launch traced here: 63.2 us
  Pallas kernels  59.3 us (93%)
  local copies, waits for them, and re-layouts  3.8 us (6%)
    pallas_call x1, Pallas kernels, table_and_tokens(): pl.pallas_call(table_kernel, name='table', out_shape=(jax.ShapeDtypeStruc...  26.8 us
    pallas_call x1, Pallas kernels, exchanged(): pl.pallas_call(exchange_kernel, name='exchange', out_shape=jax.ShapeDtype...  19 us
    pallas_call x1, Pallas kernels, convolved(): pl.pallas_call(conv_kernel, name='conv', out_shape=jax.ShapeDtypeStruct((...  12.1 us
    unnamed x13, local copies, waits for them, and re-layouts  3.11 us
    pallas_call x1, Pallas kernels, turned(): pl.pallas_call(turn_kernel, name='turn', out_shape=jax.ShapeDtypeStruct((...  1.28 us

profile of v1, /device:TPU:0, one launch (start us, length us, event | category | flops | bytes accessed | tf_op | source)
XLA Modules:
  0.0 63.2 jit_solution(10684719470321269690)
XLA Ops:
  0.0 0.7 %reshape.12.tok_ref = s32[1,768]{1,0:T(1,128)S(1)} reshape(s32[768]{0:T(1024)} %param.8) | data formatting | bytes 6144 | tf_op jit(solution)/shard_map/reshape | solution.py:196
  0.7 0.0 copy-start.4
  0.7 1.2 %copy.9 = bf16[128,3,512]{0,2,1:T(8,128)(2,1)S(1)} copy(bf16[128,3,512]{2,0,1:T(8,128)(2,1)} %param.11) | data formatting | bytes 786432 | tf_op args[3]
  1.9 0.0 copy-done.4
  1.9 0.0 copy-start
  1.9 1.2 %copy-done = bf16[512,1024]{1,0:T(8,128)(2,1)S(1)} copy-done((bf16[512,1024]{1,0:T(8,128)(2,1)S(1)}, bf16[512,1024]{1,0:T(8,128)(2,1)}, u32[]{:S(2)}) %copy-start) | copy-done | bytes 1048600
  3.2 0.0 copy-start.1
  3.2 0.0 copy-start.2
  3.2 0.0 copy-start.3
  3.2 26.8 %table.1 = (bf16[48,512]{1,0:T(8,128)(2,1)S(1)}, s32[32,1,768]{2,1,0:T(1,128)S(1)}) custom-call(s32[1,768]{1,0:T(1,128)S(1)} %reshape.12.tok_ref, bf16[512,1024]{1,0:T(8,128)(2,1)S(1)} %copy-done, f32[4,1,1024]{2,1,0:T(1,128)S(1)} %bitcast.6, bf16[3,512,128]{2,1,0:T(8,128)(2,1)S(1)} %bitcast.5), custom_call_target="tpu_custom_call" | custom-call | tf_op jit(solution)/shard_map/table/pallas_call | solution.py:174
  30.0 0.0 copy-start.5
  30.0 0.0 copy-done.1
  30.0 0.0 copy-done.2
  30.1 0.0 copy-done.3
  30.1 0.6 %copy-done.5 = f32[512]{0:T(512)S(1)} copy-done((f32[512]{0:T(512)S(1)}, f32[512]{0:T(512)}, u32[]{:S(2)}) %copy-start.5) | copy-done | bytes 2072
  30.7 12.1 %conv.1 = bf16[1536,256]{1,0:T(8,128)(2,1)S(1)} custom-call(bf16[48,512]{1,0:T(8,128)(2,1)S(1)} %get-tuple-element.7.table_ref, s32[32,1,768]{2,1,0:T(1,128)S(1)} %get-tuple-element.8.tokens_ref, f32[3,3,512]{2,1,0:T(4,128)S(1)} %copy-done.3, f32[16,512]{1,0:T(8,128)S(1)} %copy-done.1, f32[16,512]{1,0:T(8,128)S(1)} %copy-done.2, f32[1,512]{1,0:T(1,128)S(1)} %bitcast.7), custom_call_target="tpu_custom_call" | custom-call | tf_op jit(solution)/shard_map/conv/pallas_call | solution.py:316
  42.8 19.0 %exchange.1.got_ref = bf16[3,512,256]{2,1,0:T(8,128)(2,1)S(1)} custom-call(bf16[32,3,16,256]{3,2,1,0:T(8,128)(2,1)S(1)} %bitcast.4), custom_call_target="tpu_custom_call" | custom-call | tf_op jit(solution)/shard_map/exchange/pallas_call | solution.py:366
  61.9 1.3 %turn.1 = bf16[768,512]{1,0:T(8,128)(2,1)} custom-call(bf16[3,512,256]{2,1,0:T(8,128)(2,1)S(1)} %exchange.1.got_ref), custom_call_target="tpu_custom_call" | custom-call | tf_op jit(solution)/shard_map/turn/pallas_call | solution.py:389
Async XLA Ops:
  0.7 1.2 %copy-start.4 = (f32[4096]{0:T(1024)S(1)}, f32[4096]{0:T(1024)}, u32[]{:S(2)}) copy-start(f32[4096]{0:T(1024)} %param.10) | copy-start | bytes 49156
  1.9 1.2 %copy-start = (bf16[512,1024]{1,0:T(8,128)(2,1)S(1)}, bf16[512,1024]{1,0:T(8,128)(2,1)}, u32[]{:S(2)}) copy-start(bf16[512,1024]{1,0:T(8,128)(2,1)} %embed_ref.1) | copy-start | bytes 3145732
  3.2 26.9 %copy-start.1 = (f32[16,512]{1,0:T(8,128)S(1)}, f32[16,512]{1,0:T(8,128)}, u32[]{:S(2)}) copy-start(f32[16,512]{1,0:T(8,128)} %residue_ref.1) | copy-start | bytes 98308
  3.2 26.9 %copy-start.2 = (f32[16,512]{1,0:T(8,128)S(1)}, f32[16,512]{1,0:T(8,128)}, u32[]{:S(2)}) copy-start(f32[16,512]{1,0:T(8,128)} %decay_ref.1) | copy-start | bytes 98308
  3.2 26.9 %copy-start.3 = (f32[3,3,512]{2,1,0:T(4,128)S(1)}, f32[3,3,512]{2,1,0:T(4,128)}, u32[]{:S(2)}) copy-start(f32[3,3,512]{2,1,0:T(4,128)} %taps_ref.1) | copy-start | bytes 55300
  30.0 0.7 %copy-start.5 = (f32[512]{0:T(512)S(1)}, f32[512]{0:T(512)}, u32[]{:S(2)}) copy-start(f32[512]{0:T(512)} %param.15) | copy-start | bytes 6148

commit v2 on v1

v2 whole, which is shorter than its diff:
```python
import functools

import jax
import jax.numpy as jnp
from jax import lax
from jax.experimental import pallas as pl
from jax.experimental.pallas import tpu as pltpu
from jax.sharding import PartitionSpec as P

MESH = pl.DeviceIdType.MESH
EPS = 1e-06
VMEM_LIMIT = 48 * 1024 * 1024

CTX, CHAN, PLANE = 32, 4, 8
OWN = 16
SEG = 256
SEGS = 96
PER = 3
PART = 24
HALF = 128
MODES = 16
PAIRS = OWN * MODES
NT = (((1,), (1,)), ((), ()))
HIGHEST = lax.Precision.HIGHEST


def dot(a, b):
    return jnp.dot(a, b, preferred_element_type=jnp.float32)


def high_low(x):
    high = x.astype(jnp.bfloat16)
    return high, (x - high.astype(jnp.float32)).astype(jnp.bfloat16)


def send(src, dst, send_sem, recv_sem, i, c):
    return pltpu.make_async_remote_copy(
        src_ref=src, dst_ref=dst, send_sem=send_sem, recv_sem=recv_sem, device_id=(i, c), device_id_type=MESH
    )


def load_own(row_refs, lanes_from, shift):
    rows = [ref[:, pl.ds(lanes_from, HALF)] for ref in row_refs]
    return [pltpu.roll(array, shift, axis=1) for array in rows]


def filter_tables(decay, weight, toeplitz, gather, spread):
    f32, bf16 = jnp.float32, jnp.bfloat16
    decay_turned = jnp.transpose(decay)[:OWN]
    weight_turned = jnp.transpose(weight)[:OWN]
    lane = lax.broadcasted_iota(jnp.int32, (OWN, HALF), 1).astype(f32)
    near = jnp.zeros((OWN, HALF), f32)
    far = jnp.zeros((OWN, HALF), f32)
    for m in range(MODES):
        rate = jnp.broadcast_to(decay_turned[:, m : m + 1], (OWN, HALF))
        height = jnp.broadcast_to(weight_turned[:, m : m + 1], (OWN, HALF))
        near = near + height * jnp.exp(-rate * lane)
        far = far + height * jnp.exp(-rate * (lane + float(HALF)))
    causal = lax.broadcasted_iota(jnp.int32, (HALF, HALF), 1) >= lax.broadcasted_iota(jnp.int32, (HALF, HALF), 0)
    for ch in range(OWN):
        near_rolled = pltpu.roll(
            jnp.broadcast_to(near[ch : ch + 1], (HALF, HALF)), 0, axis=1, stride=1, stride_axis=0
        )
        far_rolled = pltpu.roll(
            jnp.broadcast_to(far[ch : ch + 1], (HALF, HALF)), 0, axis=1, stride=1, stride_axis=0
        )
        diagonal = jnp.where(causal, near_rolled, 0.0).astype(bf16)
        toeplitz[ch, :HALF, :HALF] = diagonal
        toeplitz[ch, HALF:, HALF:] = diagonal
        toeplitz[ch, :HALF, HALF:] = jnp.where(causal, far_rolled, near_rolled).astype(bf16)
        toeplitz[ch, HALF:, :HALF] = jnp.zeros((HALF, HALF), bf16)

    pick = (
        lax.broadcasted_iota(jnp.int32, (HALF, PAIRS), 0)
        == lax.broadcasted_iota(jnp.int32, (HALF, PAIRS), 1) // MODES
    ).astype(f32)
    own_mode = (
        lax.broadcasted_iota(jnp.int32, (MODES, PAIRS), 0)
        == lax.broadcasted_iota(jnp.int32, (MODES, PAIRS), 1) % MODES
    )

    def pair_row(array):
        wide = jnp.dot(array, pick, precision=HIGHEST, preferred_element_type=f32)
        return jnp.sum(jnp.where(own_mode, wide, 0.0), axis=0, keepdims=True)

    decay_row = pair_row(decay)
    decay_column = jnp.transpose(jnp.broadcast_to(decay_row, (HALF, PAIRS)))
    weight_column = jnp.transpose(jnp.broadcast_to(pair_row(weight), (HALF, PAIRS)))
    to_end = (SEG - 1 - lax.broadcasted_iota(jnp.int32, (SEG, PAIRS), 0)).astype(f32)
    gather[:SEG], gather[SEG:] = high_low(jnp.exp(-decay_row * to_end))
    for half in range(2):
        lanes = slice(half * HALF, (half + 1) * HALF)
        after = lax.broadcasted_iota(jnp.int32, (PAIRS, HALF), 1).astype(f32) + float(half * HALF + 1)
        high, low = high_low(weight_column * jnp.exp(-decay_column * after))
        spread[:PAIRS, lanes] = high
        spread[PAIRS : 2 * PAIRS, lanes] = high
        spread[2 * PAIRS :, lanes] = low
    return decay_row


def short_filter_and_gate(table_ref, tokens_ref, taps_ref, carried_ref, query_ref):
    f32, bf16 = jnp.float32, jnp.bfloat16
    table = jnp.concatenate([table_ref[:, :SEG], table_ref[:, SEG:]], axis=0)
    entry = lax.broadcasted_iota(jnp.int32, (SEG, SEG), 0).astype(f32).astype(bf16)
    lane = lax.broadcasted_iota(jnp.int32, (3 * OWN, HALF), 1)
    one, zero = jnp.ones((), bf16), jnp.zeros((), bf16)

    def block(g, before):
        for part in range(PER):
            ids = tokens_ref[g, :, part * SEG : (part + 1) * SEG]
            chosen = (ids & (SEG - 1)).astype(f32).astype(bf16)
            both = dot(table, jnp.where(entry == chosen, one, zero))
            projected = jnp.where(ids >= SEG, both[3 * OWN :], both[: 3 * OWN])
            at = pl.ds(g * PER + part, OWN, stride=SEGS)
            for half in range(2):
                here = projected[:, half * HALF : (half + 1) * HALF]
                turned = (pltpu.roll(here, 1, axis=1), pltpu.roll(here, 2, axis=1))
                branches = (
                    taps_ref[0] * here
                    + taps_ref[1] * jnp.where(lane < 1, before[0], turned[0])
                    + taps_ref[2] * jnp.where(lane < 2, before[1], turned[1])
                )
                before = turned
                carried = branches[OWN : 2 * OWN] * branches[2 * OWN :]
                carried_ref[half, at, :] = carried.astype(bf16).astype(f32)
                query_ref[half, at, :] = branches[:OWN]
        return before

    nothing = jnp.zeros((3 * OWN, HALF), f32)
    lax.fori_loop(0, SEGS // PER, block, (nothing, nothing), unroll=UNROLL)


UNROLL = 8


def both_halves(ref, rows):
    return jnp.concatenate([ref[half, rows, :] for half in range(2)], axis=1)


def segment_states(carried_ref, gather, decay_row, state_ref):
    f32, bf16 = jnp.float32, jnp.bfloat16
    channel_of = lax.broadcasted_iota(jnp.int32, (SEGS, PAIRS), 1) // MODES
    added = jnp.zeros((SEGS, PAIRS), f32)
    group = 4
    for first in range(0, OWN, group):
        signal = both_halves(carried_ref, slice(first * SEGS, (first + group) * SEGS)).astype(bf16)
        enters = dot(jnp.concatenate([signal, signal], axis=1), gather[...])
        for ch in range(group):
            added = added + jnp.where(channel_of == first + ch, enters[ch * SEGS : (ch + 1) * SEGS], 0.0)

    def later(x, by):
        return jnp.concatenate([jnp.zeros((by, PAIRS), f32), x[: SEGS - by]], axis=0)

    state = later(added, 1)
    by = 1
    while by < SEGS:
        state = state + jnp.exp(-decay_row * float(SEG * by)) * later(state, by)
        by *= 2
    state_ref[...] = state


def outputs_of_part(q, carried_ref, query_ref, state_ref, toeplitz, spread, skip_ref, result, ready):
    f32, bf16 = jnp.float32, jnp.bfloat16
    first = pl.multiple_of(q * PART, PART)
    high, low = high_low(state_ref[pl.ds(first, PART), :])
    channel_of = lax.broadcasted_iota(jnp.int32, (PART, PAIRS), 1) // MODES
    modes = jnp.concatenate([high, low, high], axis=1)
    channels = jnp.concatenate([channel_of] * 3, axis=1)
    zero = jnp.zeros((), bf16)
    for ch in range(OWN):
        rows = pl.ds(pl.multiple_of(ch * SEGS + first, 8), PART)
        carried = both_halves(carried_ref, rows)
        conv = dot(carried.astype(bf16), toeplitz[ch])
        conv = conv + dot(jnp.where(channels == ch, modes, zero), spread[...])
        gated = both_halves(query_ref, rows) * (conv + skip_ref[ch : ch + 1] * carried)
        for half in range(2):
            result[half, pl.ds(ch, PART, stride=OWN), :] = gated[:, half * HALF : (half + 1) * HALF]
    block = both_halves(result, slice(None)).astype(bf16)
    ready[pl.ds(q * PLANE, PLANE)] = block.reshape(PLANE, PER, OWN, SEG)


def main_kernel(
    tok_hbm, embed_hbm, gain_hbm, weight_hbm, taps_hbm, residue_hbm, decay_hbm, skip_hbm, got_ref,
    tok, embed, gain, weight, taps_all, residue, decay, skip_all,
    turned_weight, got_weight, got_square, scaled, part, part_send, part_got, tokens, table,
    toeplitz, gather, spread, taps, skip, carried, query, state, result, ready,
    in_sem, w_send, w_recv, t_send, t_recv, s_send, s_recv, p_send, p_recv, o_send, o_recv,
):
    f32, bf16 = jnp.float32, jnp.bfloat16
    i, c = lax.axis_index("ctx"), lax.axis_index("chan")
    plane, place = i // PLANE, i % PLANE

    loads = [
        pltpu.make_async_copy(src, dst, in_sem.at[n])
        for n, (src, dst) in enumerate(
            (
                (weight_hbm, weight), (tok_hbm, tok), (embed_hbm, embed), (gain_hbm, gain),
                (taps_hbm, taps_all), (residue_hbm, residue), (decay_hbm, decay), (skip_hbm, skip_all),
            )
        )
    ]
    for load in loads:
        load.start()

    barrier = pltpu.get_barrier_semaphore()

    @pl.loop(0, CTX)
    def _(j):
        row, col = c * PLANE + j % PLANE, j // PLANE

        @pl.when(jnp.logical_or(row != i, col != c))
        def _():
            pl.semaphore_signal(barrier, inc=1, device_id=(row, col), device_id_type=MESH)

    @pl.loop(1, CTX)
    def _(j):
        pl.semaphore_signal(barrier, inc=1, device_id=((i + j) % CTX, c), device_id_type=MESH)

    for d in range(1, CHAN):
        pl.semaphore_signal(barrier, inc=1, device_id=(i, (c + d) % CHAN), device_id_type=MESH)

    loads[0].wait()
    for b in range(3):
        turned_weight[b] = jnp.transpose(weight[b])
    loads[1].wait()
    tokens[i] = tok[...].reshape(1, tok.shape[0])

    pl.semaphore_wait(barrier, CTX - jnp.where(plane == c, 1, 0) + (CTX - 1) + (CHAN - 1))

    def weight_copy(j):
        to = (i + j) % CTX
        return send(
            turned_weight.at[:, pl.ds(to * OWN, OWN), :],
            got_weight.at[c, :, :, pl.ds(place * HALF, HALF)],
            w_send.at[j],
            w_recv.at[c * PLANE + place],
            to,
            plane,
        )

    def token_copy(j):
        return send(tokens.at[i], tokens.at[i], t_send.at[j], t_recv.at[i], (i + j) % CTX, c)

    @pl.loop(1, CTX)
    def _(j):
        weight_copy(j).start()

    self_copy = pltpu.make_async_copy(
        turned_weight.at[:, pl.ds(i * OWN, OWN), :],
        got_weight.at[c, :, :, pl.ds(place * HALF, HALF)],
        w_recv.at[c * PLANE + place],
    )

    @pl.when(plane == c)
    def _():
        self_copy.start()

    @pl.when(plane != c)
    def _():
        weight_copy(0).start()

    @pl.loop(1, CTX)
    def _(j):
        token_copy(j).start()

    loads[2].wait()
    loads[3].wait()
    wide = embed[...].astype(f32)
    feats = embed.shape[1]
    square_high, square_low = high_low(wide * wide)
    ones = jnp.ones((8, feats), bf16)
    squares = lax.dot_general(ones, square_high, NT, preferred_element_type=f32)
    got_square[c] = squares + lax.dot_general(ones, square_low, NT, preferred_element_type=f32)

    def square_copy(d):
        return send(got_square.at[c], got_square.at[c], s_send.at[d], s_recv.at[c], i, (c + d) % CHAN)

    for d in range(1, CHAN):
        square_copy(d).start()
    scaled[...] = (wide * gain[pl.ds(c * feats, feats)].reshape(1, feats)).astype(bf16)

    for load in loads[4:]:
        load.wait()
    lanes_from = pl.multiple_of((i // PLANE) * HALF, HALF)
    shift = lax.rem(HALF - place * OWN, HALF)
    decay_own, residue_own = load_own([decay, residue], lanes_from, shift)
    weight_own = residue_own * jnp.sqrt(decay_own)
    decay_row = filter_tables(decay_own, weight_own, toeplitz, gather, spread)
    for j in range(3):
        (rows,) = load_own([taps_all.at[j]], lanes_from, shift)
        padded = jnp.concatenate([rows, jnp.zeros((5, HALF), f32)], axis=0)
        columns = jnp.transpose(padded)[:OWN]
        for b in range(3):
            taps[j, b * OWN : (b + 1) * OWN, :] = jnp.broadcast_to(columns[:, b : b + 1], (OWN, HALF))
    skip_row = pltpu.roll(
        jnp.broadcast_to(skip_all[pl.ds(lanes_from, HALF)].reshape(1, HALF), (8, HALF)), shift, axis=1
    )
    skip_column = jnp.transpose(skip_row)[:OWN, 0:1]
    skip[...] = jnp.broadcast_to(skip_column, (OWN, SEG))

    @pl.loop(0, CTX)
    def _(s):
        pltpu.make_async_copy(
            turned_weight.at[:, pl.ds(0, OWN), :],
            got_weight.at[s // PLANE, :, :, pl.ds((s % PLANE) * HALF, HALF)],
            w_recv.at[s],
        ).wait()

    def part_copy(d):
        to = (c + d) % CHAN
        return send(part_send.at[to], part_got.at[c], p_send.at[d], p_recv.at[c], i, to)

    product = lax.dot_general(
        got_weight[...].reshape(CHAN * 3 * OWN, feats), scaled[...], NT, preferred_element_type=f32
    )
    part[...] = product.reshape(part.shape)
    part_send[...] = product.astype(bf16).reshape(part.shape)
    for d in range(1, CHAN):
        part_copy(d).start()
    mean = got_square[c]
    for d in range(1, CHAN):
        source = (c + d) % CHAN
        send(got_square.at[c], got_square.at[source], s_send.at[d], s_recv.at[source], i, source).wait_recv()
        mean = mean + got_square[source]
    scale = lax.rsqrt(mean[0:1] * (1.0 / (CHAN * feats)) + EPS)

    @pl.loop(1, CTX)
    def _(j):
        s = (i + j) % CTX
        pltpu.make_async_copy(tokens.at[i], tokens.at[s], t_recv.at[s]).wait()

    total = part[c]
    for d in range(1, CHAN):
        source = (c + d) % CHAN
        send(part_send.at[0], part_got.at[source], p_send.at[d], p_recv.at[source], i, source).wait_recv()
        total = total + part_got[source].astype(f32)
    table[...] = (total * scale).astype(bf16)

    short_filter_and_gate(table, tokens, taps, carried, query)
    segment_states(carried, gather, decay_row, state)

    def out_copy(to, slot):
        return send(
            ready.at[to], got_ref.at[:, pl.ds(i * OWN, OWN), :], o_send.at[slot], o_recv.at[i], to, c
        )

    own_out = pltpu.make_async_copy(ready.at[i], got_ref.at[:, pl.ds(i * OWN, OWN), :], o_recv.at[i])

    @pl.loop(0, CTX // PLANE)
    def _(step):
        q = (plane + 1 + step) % (CTX // PLANE)
        outputs_of_part(q, carried, query, state, toeplitz, spread, skip, result, ready)

        @pl.loop(0, PLANE)
        def _(n):
            to = q * PLANE + (place + n) % PLANE

            @pl.when(to != i)
            def _():
                out_copy(to, to).start()

            @pl.when(to == i)
            def _():
                own_out.start()

    @pl.loop(0, CTX)
    def _(s):
        pltpu.make_async_copy(ready.at[0], got_ref.at[:, pl.ds(s * OWN, OWN), :], o_recv.at[s]).wait()

    @pl.loop(1, CTX)
    def _(j):
        weight_copy(j).wait_send()
        token_copy(j).wait_send()
        out_copy((i + j) % CTX, (i + j) % CTX).wait_send()

    @pl.when(plane != c)
    def _():
        weight_copy(0).wait_send()

    for d in range(1, CHAN):
        square_copy(d).wait_send()
        part_copy(d).wait_send()


def gathered(
    token_ids, embed_table, norm_gain, in_weight, short_filter, residue, decay_rate, skip_bias
):
    f32, bf16 = jnp.float32, jnp.bfloat16
    rows = token_ids.shape[0]
    vocab, feats = embed_table.shape
    chans = decay_rate.shape[1]
    weight = jnp.transpose(in_weight, (1, 0, 2))
    operands = (token_ids, embed_table, norm_gain, weight, short_filter, residue, decay_rate, skip_bias)
    dma, vmem = pltpu.SemaphoreType.DMA, pltpu.VMEM
    return pl.pallas_call(
        main_kernel,
        name="hyena",
        out_shape=jax.ShapeDtypeStruct((PER, CTX * OWN, SEG), bf16),
        in_specs=[pl.BlockSpec(memory_space=pltpu.HBM)] * len(operands),
        out_specs=pl.BlockSpec(memory_space=pltpu.VMEM),
        scratch_shapes=[
            vmem(token_ids.shape, jnp.int32),
            vmem(embed_table.shape, bf16),
            vmem(norm_gain.shape, f32),
            vmem(weight.shape, bf16),
            vmem(short_filter.shape, f32),
            vmem(residue.shape, f32),
            vmem(decay_rate.shape, f32),
            vmem(skip_bias.shape, f32),
            vmem((3, chans, in_weight.shape[0]), bf16),
            vmem((CHAN, 3, OWN, feats), bf16),
            vmem((CHAN, 8, vocab), f32),
            vmem((vocab, feats), bf16),
            vmem((CHAN, 3 * OWN, vocab), f32),
            vmem((CHAN, 3 * OWN, vocab), bf16),
            vmem((CHAN, 3 * OWN, vocab), bf16),
            vmem((CTX, 1, rows), jnp.int32),
            vmem((3 * OWN, vocab), bf16),
            vmem((OWN, SEG, SEG), bf16),
            vmem((2 * SEG, PAIRS), bf16),
            vmem((3 * PAIRS, SEG), bf16),
            vmem((3, 3 * OWN, HALF), f32),
            vmem((OWN, SEG), f32),
            vmem((2, OWN * SEGS, HALF), f32),
            vmem((2, OWN * SEGS, HALF), f32),
            vmem((SEGS, PAIRS), f32),
            vmem((2, PART * OWN, HALF), f32),
            vmem((CTX, PER, OWN, SEG), bf16),
            dma((8,)),
            dma((CTX,)), dma((CTX,)), dma((CTX,)), dma((CTX,)),
            dma((CHAN,)), dma((CHAN,)), dma((CHAN,)), dma((CHAN,)),
            dma((CTX,)), dma((CTX,)),
        ],
        compiler_params=pltpu.CompilerParams(
            collective_id=0, has_side_effects=True, vmem_limit_bytes=VMEM_LIMIT
        ),
    )(*operands)


def turn_kernel(got_ref, out_ref):
    unit = (
        lax.broadcasted_iota(jnp.int32, (SEG, SEG), 0) == lax.broadcasted_iota(jnp.int32, (SEG, SEG), 1)
    ).astype(jnp.bfloat16)
    for g in range(PER):
        turned = lax.dot_general(unit, got_ref[g], NT, preferred_element_type=jnp.float32)
        out_ref[g * SEG : (g + 1) * SEG, :] = turned.astype(jnp.bfloat16)


def turned(got):
    return pl.pallas_call(
        turn_kernel,
        name="turn",
        out_shape=jax.ShapeDtypeStruct((PER * SEG, got.shape[1]), jnp.bfloat16),
        in_specs=[pl.BlockSpec(memory_space=pltpu.VMEM)],
        out_specs=pl.BlockSpec(memory_space=pltpu.VMEM),
        compiler_params=pltpu.CompilerParams(vmem_limit_bytes=VMEM_LIMIT),
    )(got)


def per_device(*arrays):
    return turned(gathered(*arrays))


def solution(mesh):
    return jax.shard_map(
        per_device,
        mesh=mesh,
        in_specs=(
            P("ctx"),
            P(None, "chan"),
            P(),
            P("ctx", None, "chan"),
            P(None, None, "chan"),
            P(None, "chan"),
            P(None, "chan"),
            P("chan"),
        ),
        out_specs=P("ctx", "chan"),
        check_vma=False,
    )
```

time: 64.1 us -> 57.9 us (0.903)
  Pallas kernels: 59.3 us -> 50.3 us
  local copies, waits for them, and re-layouts: 3.8 us -> 6.56 us
    pallas_call x3 -> x1, Pallas kernels: 58 us -> 49 us  [gathered(): pl.pallas_call(main_kernel, name='hyena', out_shape=jax.ShapeDtypeStruct(...]
    unnamed x13 -> x16, local copies, waits for them, and re-layouts: 3.11 us -> 6.56 us
    reshape x1 -> x0, local copies, waits for them, and re-layouts: 0.69 us -> none  [table_and_tokens(): token_ids.reshape(1, rows)]
where the time goes in v2:
time: 57.9 us; the launch traced here: 56.9 us
  Pallas kernels  50.3 us (87%)
  local copies, waits for them, and re-layouts  6.56 us (11%)
    pallas_call x1, Pallas kernels, gathered(): pl.pallas_call(main_kernel, name='hyena', out_shape=jax.ShapeDtypeStruct(...  49 us
    unnamed x16, local copies, waits for them, and re-layouts  6.56 us
    pallas_call x1, Pallas kernels, turned(): pl.pallas_call(turn_kernel, name='turn', out_shape=jax.ShapeDtypeStruct((...  1.28 us

profile of v2, /device:TPU:0, one launch (start us, length us, event | category | flops | bytes accessed | tf_op | source)
XLA Modules:
  0.0 56.9 jit_solution(7748801018521858700)
XLA Ops:
  0.0 0.0 copy-start
  0.0 1.2 %copy-done = bf16[512,1024]{1,0:T(8,128)(2,1)S(1)} copy-done((bf16[512,1024]{1,0:T(8,128)(2,1)S(1)}, bf16[512,1024]{1,0:T(8,128)(2,1)}, u32[]{:S(2)}) %copy-start) | copy-done | bytes 1048600
  1.2 0.0 copy-start.1
  1.2 1.0 %copy-done.1 = bf16[128,3,512]{2,0,1:T(8,128)(2,1)S(1)} copy-done((bf16[128,3,512]{2,0,1:T(8,128)(2,1)S(1)}, bf16[128,3,512]{2,0,1:T(8,128)(2,1)}, u32[]{:S(2)}) %copy-start.1) | copy-done | bytes 393240
  2.2 0.0 copy-start.2
  2.2 0.8 %copy-done.2 = f32[16,512]{1,0:T(8,128)S(1)} copy-done((f32[16,512]{1,0:T(8,128)S(1)}, f32[16,512]{1,0:T(8,128)}, u32[]{:S(2)}) %copy-start.2) | copy-done | bytes 32792
  3.0 0.0 copy-start.3
  3.0 0.8 %copy-done.3 = f32[16,512]{1,0:T(8,128)S(1)} copy-done((f32[16,512]{1,0:T(8,128)S(1)}, f32[16,512]{1,0:T(8,128)}, u32[]{:S(2)}) %copy-start.3) | copy-done | bytes 32792
  3.7 0.0 copy-start.4
  3.7 0.7 %copy-done.4 = f32[3,3,512]{2,1,0:T(4,128)S(1)} copy-done((f32[3,3,512]{2,1,0:T(4,128)S(1)}, f32[3,3,512]{2,1,0:T(4,128)}, u32[]{:S(2)}) %copy-start.4) | copy-done | bytes 18456
  4.5 0.0 copy-start.5
  4.5 0.7 %copy-done.5 = f32[4096]{0:T(1024)S(1)} copy-done((f32[4096]{0:T(1024)S(1)}, f32[4096]{0:T(1024)}, u32[]{:S(2)}) %copy-start.5) | copy-done | bytes 16408
  5.2 0.0 copy-start.6
  5.2 0.7 %copy-done.6 = s32[768]{0:T(1024)S(1)} copy-done((s32[768]{0:T(1024)S(1)}, s32[768]{0:T(1024)}, u32[]{:S(2)}) %copy-start.6) | copy-done | bytes 3096
  5.9 0.0 copy-start.7
  5.9 0.7 %copy-done.7 = f32[512]{0:T(512)S(1)} copy-done((f32[512]{0:T(512)S(1)}, f32[512]{0:T(512)}, u32[]{:S(2)}) %copy-start.7) | copy-done | bytes 2072
  6.6 49.0 %hyena.1.got_ref = bf16[3,512,256]{2,1,0:T(8,128)(2,1)S(1)} custom-call(s32[768]{0:T(1024)S(1)} %copy-done.6, bf16[512,1024]{1,0:T(8,128)(2,1)S(1)} %copy-done, f32[4096]{0:T(1024)S(1)} %copy-done.5, bf16[3,128,512]{2,1,0:T(8,128)(2,1)S(1)} %bitcast.1, f32[3,3,512]{2,1,0:T(4,128)S(1)} %copy-done.4, f32[16,512]{1,0:T(8,128)S(1)} %copy-done.2, ...), custom_call_target="tpu_custom_call" | custom-call | tf_op jit(solution)/shard_map/hyena/pallas_call | solution.py:395
  55.6 1.3 %turn.1 = bf16[768,512]{1,0:T(8,128)(2,1)} custom-call(bf16[3,512,256]{2,1,0:T(8,128)(2,1)S(1)} %hyena.1.got_ref), custom_call_target="tpu_custom_call" | custom-call | tf_op jit(solution)/shard_map/turn/pallas_call | solution.py:450
Async XLA Ops:
  0.0 1.2 %copy-start = (bf16[512,1024]{1,0:T(8,128)(2,1)S(1)}, bf16[512,1024]{1,0:T(8,128)(2,1)}, u32[]{:S(2)}) copy-start(bf16[512,1024]{1,0:T(8,128)(2,1)} %embed_hbm.1) | copy-start | bytes 3145732
  1.2 1.0 %copy-start.1 = (bf16[128,3,512]{2,0,1:T(8,128)(2,1)S(1)}, bf16[128,3,512]{2,0,1:T(8,128)(2,1)}, u32[]{:S(2)}) copy-start(bf16[128,3,512]{2,0,1:T(8,128)(2,1)} %param.11) | copy-start | bytes 1179652
  2.2 0.8 %copy-start.2 = (f32[16,512]{1,0:T(8,128)S(1)}, f32[16,512]{1,0:T(8,128)}, u32[]{:S(2)}) copy-start(f32[16,512]{1,0:T(8,128)} %residue_hbm.1) | copy-start | bytes 98308
  3.0 0.8 %copy-start.3 = (f32[16,512]{1,0:T(8,128)S(1)}, f32[16,512]{1,0:T(8,128)}, u32[]{:S(2)}) copy-start(f32[16,512]{1,0:T(8,128)} %decay_hbm.1) | copy-start | bytes 98308
  3.7 0.7 %copy-start.4 = (f32[3,3,512]{2,1,0:T(4,128)S(1)}, f32[3,3,512]{2,1,0:T(4,128)}, u32[]{:S(2)}) copy-start(f32[3,3,512]{2,1,0:T(4,128)} %taps_hbm.1) | copy-start | bytes 55300
  4.5 0.7 %copy-start.5 = (f32[4096]{0:T(1024)S(1)}, f32[4096]{0:T(1024)}, u32[]{:S(2)}) copy-start(f32[4096]{0:T(1024)} %gain_hbm.1) | copy-start | bytes 49156
  5.2 0.7 %copy-start.6 = (s32[768]{0:T(1024)S(1)}, s32[768]{0:T(1024)}, u32[]{:S(2)}) copy-start(s32[768]{0:T(1024)} %tok_hbm.1) | copy-start | bytes 9220
  5.9 0.7 %copy-start.7 = (f32[512]{0:T(512)S(1)}, f32[512]{0:T(512)}, u32[]{:S(2)}) copy-start(f32[512]{0:T(512)} %skip_hbm.1) | copy-start | bytes 6148

commit v3 on v2

v3 whole, which is shorter than its diff:
```python
import functools

import jax
import jax.numpy as jnp
from jax import lax
from jax.experimental import pallas as pl
from jax.experimental.pallas import tpu as pltpu
from jax.sharding import PartitionSpec as P

MESH = pl.DeviceIdType.MESH
EPS = 1e-06
VMEM_LIMIT = 60 * 1024 * 1024

CTX, CHAN, PLANE = 32, 4, 8
OWN = 16
SEG = 256
SEGS = 96
PER = 3
PART = 24
HALF = 128
MODES = 16
PAIRS = OWN * MODES
FEW = 8
FEWS = FEW * MODES
WEIGHT_ROWS = ((0, 32), (32, 16))
TABLE_ROWS = ((0, 8, 16), (32, 24, 40))
NT = (((1,), (1,)), ((), ()))
HIGHEST = lax.Precision.HIGHEST


def dot(a, b):
    return jnp.dot(a, b, preferred_element_type=jnp.float32)


def high_low(x):
    high = x.astype(jnp.bfloat16)
    return high, (x - high.astype(jnp.float32)).astype(jnp.bfloat16)


def send(src, dst, send_sem, recv_sem, i, c):
    return pltpu.make_async_remote_copy(
        src_ref=src, dst_ref=dst, send_sem=send_sem, recv_sem=recv_sem, device_id=(i, c), device_id_type=MESH
    )


def load_own(row_refs, lanes_from, shift):
    rows = [ref[:, pl.ds(lanes_from, HALF)] for ref in row_refs]
    return [pltpu.roll(array, shift, axis=1) for array in rows]


def filter_tables(decay, weight, gather, reach):
    f32, bf16 = jnp.float32, jnp.bfloat16
    decay_turned = jnp.transpose(decay)[:OWN]
    weight_turned = jnp.transpose(weight)[:OWN]
    lane = lax.broadcasted_iota(jnp.int32, (OWN, HALF), 1).astype(f32)
    near = jnp.zeros((OWN, HALF), f32)
    far = jnp.zeros((OWN, HALF), f32)
    for m in range(MODES):
        rate = jnp.broadcast_to(decay_turned[:, m : m + 1], (OWN, HALF))
        height = jnp.broadcast_to(weight_turned[:, m : m + 1], (OWN, HALF))
        near = near + height * jnp.exp(-rate * lane)
        far = far + height * jnp.exp(-rate * (lane + float(HALF)))
    causal = lax.broadcasted_iota(jnp.int32, (HALF, HALF), 1) >= lax.broadcasted_iota(jnp.int32, (HALF, HALF), 0)
    for ch in range(OWN):
        near_rolled = pltpu.roll(
            jnp.broadcast_to(near[ch : ch + 1], (HALF, HALF)), 0, axis=1, stride=1, stride_axis=0
        )
        far_rolled = pltpu.roll(
            jnp.broadcast_to(far[ch : ch + 1], (HALF, HALF)), 0, axis=1, stride=1, stride_axis=0
        )
        diagonal = jnp.where(causal, near_rolled, 0.0).astype(bf16)
        part, top = ch // FEW, ch % FEW * SEG
        middle, end = top + HALF, top + SEG
        reach[part, top:middle, :HALF] = diagonal
        reach[part, middle:end, HALF:] = diagonal
        reach[part, top:middle, HALF:] = jnp.where(causal, far_rolled, near_rolled).astype(bf16)
        reach[part, middle:end, :HALF] = jnp.zeros((HALF, HALF), bf16)

    pick = (
        lax.broadcasted_iota(jnp.int32, (HALF, PAIRS), 0)
        == lax.broadcasted_iota(jnp.int32, (HALF, PAIRS), 1) // MODES
    ).astype(f32)
    own_mode = (
        lax.broadcasted_iota(jnp.int32, (MODES, PAIRS), 0)
        == lax.broadcasted_iota(jnp.int32, (MODES, PAIRS), 1) % MODES
    )

    def pair_row(array):
        wide = jnp.dot(array, pick, precision=HIGHEST, preferred_element_type=f32)
        return jnp.sum(jnp.where(own_mode, wide, 0.0), axis=0, keepdims=True)

    decay_row = pair_row(decay)
    decay_column = jnp.transpose(jnp.broadcast_to(decay_row, (HALF, PAIRS)))
    weight_column = jnp.transpose(jnp.broadcast_to(pair_row(weight), (HALF, PAIRS)))
    to_end = (SEG - 1 - lax.broadcasted_iota(jnp.int32, (SEG, PAIRS), 0)).astype(f32)
    entering = high_low(jnp.exp(-decay_row * to_end))
    for part in range(2):
        for n in range(2):
            gather[part, :, n * FEWS : (n + 1) * FEWS] = entering[n][:, part * FEWS : (part + 1) * FEWS]
    for half in range(2):
        lanes = slice(half * HALF, (half + 1) * HALF)
        after = lax.broadcasted_iota(jnp.int32, (PAIRS, HALF), 1).astype(f32) + float(half * HALF + 1)
        high, low = high_low(weight_column * jnp.exp(-decay_column * after))
        for part in range(2):
            rows = slice(part * FEWS, (part + 1) * FEWS)
            for n, piece in enumerate((high, high, low)):
                top = FEW * SEG + n * FEWS
                reach[part, top : top + FEWS, lanes] = piece[rows]
    return decay_row


def short_filter_and_gate(table, tokens_ref, taps_ref, carried_ref, query_ref):
    f32, bf16 = jnp.float32, jnp.bfloat16
    rows = 3 * FEW
    entry = lax.broadcasted_iota(jnp.int32, (SEG, SEG), 0).astype(f32).astype(bf16)
    lane = lax.broadcasted_iota(jnp.int32, (rows, HALF), 1)
    one, zero = jnp.ones((), bf16), jnp.zeros((), bf16)

    def block(g, before):
        for part in range(PER):
            ids = tokens_ref[g, :, part * SEG : (part + 1) * SEG]
            chosen = (ids & (SEG - 1)).astype(f32).astype(bf16)
            both = dot(table, jnp.where(entry == chosen, one, zero))
            projected = jnp.where(ids >= SEG, both[rows:], both[:rows])
            at = pl.ds(pl.multiple_of((g * PER + part) * FEW, FEW), FEW)
            for half in range(2):
                lanes = slice(half * HALF, (half + 1) * HALF)
                here = projected[:, lanes]
                turned = (pltpu.roll(here, 1, axis=1), pltpu.roll(here, 2, axis=1))
                branches = (
                    taps_ref[0] * here
                    + taps_ref[1] * jnp.where(lane < 1, before[0], turned[0])
                    + taps_ref[2] * jnp.where(lane < 2, before[1], turned[1])
                )
                before = turned
                carried = branches[FEW : 2 * FEW] * branches[2 * FEW :]
                carried_ref[at, lanes] = carried.astype(bf16).astype(f32)
                query_ref[at, lanes] = branches[:FEW]
        return before

    nothing = jnp.zeros((rows, HALF), f32)
    lax.fori_loop(0, SEGS // PER, block, (nothing, nothing), unroll=UNROLL)


UNROLL = 16


def own_pairs():
    shape = (1, FEW, FEWS)
    return lax.broadcasted_iota(jnp.int32, shape, 2) // MODES == lax.broadcasted_iota(jnp.int32, shape, 1)


def segment_states(carried_ref, gather, decay_row, state_ref):
    f32, bf16 = jnp.float32, jnp.bfloat16
    enters = dot(carried_ref[...].astype(bf16), gather[...])
    enters = (enters[:, :FEWS] + enters[:, FEWS:]).reshape(SEGS, FEW, FEWS)
    added = jnp.sum(jnp.where(own_pairs(), enters, 0.0), axis=1)

    def later(x, by):
        return jnp.concatenate([jnp.zeros((by, FEWS), f32), x[: SEGS - by]], axis=0)

    state = later(added, 1)
    by = 1
    while by < SEGS:
        state = state + jnp.exp(-decay_row * float(SEG * by)) * later(state, by)
        by *= 2
    state_ref[...] = state


def outputs_of_part(q, carried_ref, query_ref, state_ref, reach, skip_ref, ready):
    f32, bf16 = jnp.float32, jnp.bfloat16
    first = pl.multiple_of(q * PART, PART)
    rows = pl.ds(pl.multiple_of(first * FEW, FEW), PART * FEW)
    carried = carried_ref[rows, :].reshape(PART, FEW, SEG)
    channel = lax.broadcasted_iota(jnp.int32, (1, FEW, SEG), 1)
    parts = [
        jnp.where(channel == ch, carried, 0.0).reshape(PART * FEW, SEG).astype(bf16) for ch in range(FEW)
    ]
    state = jnp.where(own_pairs(), state_ref[pl.ds(first, PART), :][:, None, :], 0.0)
    high, low = high_low(state.reshape(PART * FEW, FEWS))
    conv = dot(jnp.concatenate(parts + [high, low, high], axis=1), reach[...])
    gated = query_ref[rows, :] * (conv + (skip_ref[...][None] * carried).reshape(PART * FEW, SEG))
    halves = [gated[:, half * HALF : (half + 1) * HALF].reshape(PART, 1, FEW, HALF) for half in range(2)]
    block = jnp.concatenate(halves, axis=1).reshape(PLANE, PER, 2 * FEW, HALF)
    ready[pl.ds(q * PLANE, PLANE)] = block.astype(bf16)


def main_kernel(
    tok_hbm, embed_hbm, gain_hbm, weight_hbm, taps_hbm, residue_hbm, decay_hbm, skip_hbm, got_ref,
    tok, own_tokens, embed, gain, weight, taps_all, residue, decay, skip_all,
    turned_weight, got_weight, got_square, scaled, part, part_send0, part_send1, part_got0, part_got1, tokens, table,
    gather, reach, taps, skip, carried, query, state, ready,
    in_sem, w_send, w_recv, t_send, t_recv, u_send, u_recv, s_send, s_recv, p_send, p_recv, o_send, o_recv,
):
    f32, bf16 = jnp.float32, jnp.bfloat16
    i, c = lax.axis_index("ctx"), lax.axis_index("chan")
    plane, place = i // PLANE, i % PLANE

    loads = [
        pltpu.make_async_copy(src, dst, in_sem.at[n])
        for n, (src, dst) in enumerate(
            (
                (weight_hbm, weight), (tok_hbm, tok), (embed_hbm, embed), (gain_hbm, gain),
                (taps_hbm, taps_all), (residue_hbm, residue), (decay_hbm, decay), (skip_hbm, skip_all),
            )
        )
    ]
    for load in loads:
        load.start()

    barrier = pltpu.get_barrier_semaphore()

    @pl.loop(0, CTX)
    def _(j):
        row, col = c * PLANE + j % PLANE, j // PLANE

        @pl.when(jnp.logical_or(row != i, col != c))
        def _():
            pl.semaphore_signal(barrier, inc=1, device_id=(row, col), device_id_type=MESH)

    for d in range(1, CHAN):
        pl.semaphore_signal(barrier, inc=1, device_id=(i, (c + d) % CHAN), device_id_type=MESH)

    loads[0].wait()
    eights = [jnp.transpose(weight[b].astype(f32)).reshape(CTX, 2, FEW, HALF) for b in range(3)]
    order = ((0, 0), (1, 0), (2, 0), (1, 1), (0, 1), (2, 1))
    rows = jnp.concatenate([eights[b][:, part : part + 1] for b, part in order], axis=1)
    turned_weight[...] = rows.reshape(turned_weight.shape).astype(bf16)
    loads[1].wait()
    own_tokens[...] = tok[...].reshape(1, tok.shape[0])

    pl.semaphore_wait(barrier, CTX - jnp.where(plane == c, 1, 0) + CHAN - 1)

    def weight_slices(h, to, slot):
        rows = pl.ds(*WEIGHT_ROWS[h])
        lanes = pl.ds(pl.multiple_of(slot % PLANE * HALF, HALF), HALF)
        return turned_weight.at[to, rows, :], got_weight.at[slot // PLANE, rows, lanes], w_recv.at[h, slot]

    def weight_copy(h, j):
        to = (i + j) % CTX
        src, dst, sem = weight_slices(h, to, c * PLANE + place)
        return send(src, dst, w_send.at[h, j], sem, to, plane)

    def start_weights(h):
        @pl.loop(1, CTX)
        def _(j):
            weight_copy(h, j).start()

        @pl.when(plane == c)
        def _():
            pltpu.make_async_copy(*weight_slices(h, i, c * PLANE + place)).start()

        @pl.when(plane != c)
        def _():
            weight_copy(h, 0).start()

    def wait_weights(h):
        @pl.loop(0, CTX)
        def _(slot):
            pltpu.make_async_copy(*weight_slices(h, 0, slot)).wait()

    def token_copy(n):
        to = c * PLANE + (place + n) % PLANE
        return send(own_tokens, tokens.at[i], t_send.at[n], t_recv.at[place], to, plane)

    own_token_copy = pltpu.make_async_copy(own_tokens, tokens.at[i], t_recv.at[place])

    @pl.when(plane == c)
    def _():
        own_token_copy.start()

    @pl.when(plane != c)
    def _():
        token_copy(0).start()

    @pl.loop(1, PLANE)
    def _(n):
        token_copy(n).start()

    start_weights(0)

    loads[2].wait()
    loads[3].wait()
    wide = embed[...].astype(f32)
    feats = embed.shape[1]
    square_high, square_low = high_low(wide * wide)
    ones = jnp.ones((8, feats), bf16)
    squares = lax.dot_general(ones, square_high, NT, preferred_element_type=f32)
    got_square[c] = squares + lax.dot_general(ones, square_low, NT, preferred_element_type=f32)

    def square_copy(d):
        return send(got_square.at[c], got_square.at[c], s_send.at[d], s_recv.at[c], i, (c + d) % CHAN)

    for d in range(1, CHAN):
        square_copy(d).start()
    scaled[...] = (wide * gain[pl.ds(c * feats, feats)].reshape(1, feats)).astype(bf16)

    @pl.loop(0, PLANE)
    def _(n):
        pltpu.make_async_copy(own_tokens, tokens.at[c * PLANE + n], t_recv.at[n]).wait()

    def plane_copy(source, to, d):
        block = tokens.at[pl.ds(source * PLANE, PLANE)]
        return send(block, block, u_send.at[d], u_recv.at[source], i, to)

    for d in range(1, CHAN):
        plane_copy(c, (c + d) % CHAN, d).start()

    for load in loads[4:]:
        load.wait()
    lanes_from = pl.multiple_of((i // PLANE) * HALF, HALF)
    shift = lax.rem(HALF - place * OWN, HALF)
    decay_own, residue_own = load_own([decay, residue], lanes_from, shift)
    weight_own = residue_own * jnp.sqrt(decay_own)
    decay_row = filter_tables(decay_own, weight_own, gather, reach)
    for j in range(3):
        (rows,) = load_own([taps_all.at[j]], lanes_from, shift)
        padded = jnp.concatenate([rows, jnp.zeros((5, HALF), f32)], axis=0)
        columns = jnp.transpose(padded)[:OWN]
        for b in range(3):
            wide_column = jnp.broadcast_to(columns[:, b : b + 1], (OWN, HALF))
            for h in range(2):
                taps[h, j, b * FEW : (b + 1) * FEW, :] = wide_column[h * FEW : (h + 1) * FEW]
    skip_row = pltpu.roll(
        jnp.broadcast_to(skip_all[pl.ds(lanes_from, HALF)].reshape(1, HALF), (8, HALF)), shift, axis=1
    )
    skip_column = jnp.transpose(skip_row)[:OWN, 0:1]
    skip[...] = jnp.broadcast_to(skip_column, (OWN, SEG)).reshape(2, FEW, SEG)

    start_weights(1)

    near, far = (c // 2) * 2, 2 - (c // 2) * 2
    other = c + 1 - 2 * (c % 2)
    part_send, part_got = (part_send0, part_send1), (part_got0, part_got1)

    def part_copy(h, to, d):
        return send(part_send[h].at[to], part_got[h].at[c], p_send.at[h, d], p_recv.at[h, c], i, to)

    def products(h, first):
        top, count = WEIGHT_ROWS[h]
        weights = got_weight[pl.ds(first, 2), pl.ds(top, count), :].reshape(2 * count, feats)
        product = lax.dot_general(weights, scaled[...], NT, preferred_element_type=f32)
        return product.reshape(2, count, product.shape[1])

    def start_parts(h):
        top, count = WEIGHT_ROWS[h]
        part_send[h][pl.ds(far, 2)] = products(h, far).astype(bf16)
        part_copy(h, far, 0).start()
        part_copy(h, far + 1, 1).start()
        product = products(h, near)
        part[:, top : top + count, :] = product
        part_send[h][pl.ds(near, 2)] = product.astype(bf16)
        part_copy(h, other, 2).start()

    def finish_parts(h, scale):
        top, count = WEIGHT_ROWS[h]
        total = part[c % 2, top : top + count, :]
        for d in range(1, CHAN):
            source = (c + d) % CHAN
            send(
                part_send[h].at[0], part_got[h].at[source], p_send.at[h, d], p_recv.at[h, source], i, source
            ).wait_recv()
            total = total + part_got[h][source].astype(f32)
        table[top : top + count, :] = (total * scale).astype(bf16).astype(f32)

    def branches_of(h):
        rows = jnp.concatenate([table[top : top + FEW, :] for top in TABLE_ROWS[h]], axis=0)
        halves = jnp.concatenate([rows[:, :SEG], rows[:, SEG:]], axis=0).astype(bf16)
        short_filter_and_gate(halves, tokens, taps.at[h], carried.at[h], query.at[h])

    def out_slot(h, source):
        return got_ref.at[h, :, pl.ds(pl.multiple_of(source * OWN, OWN), OWN), :], o_recv.at[h, source]

    def out_copy(h, to):
        dst, sem = out_slot(h, i)
        return send(ready.at[h, to], dst, o_send.at[h, to], sem, to, c)

    def start_outputs(h):
        segment_states(carried.at[h], gather.at[h], decay_row[:, h * FEWS : (h + 1) * FEWS], state.at[h])

        @pl.loop(0, CTX // PLANE)
        def _(step):
            q = (plane + 1 + step) % (CTX // PLANE)
            outputs_of_part(
                q, carried.at[h], query.at[h], state.at[h], reach.at[h], skip.at[h], ready.at[h]
            )

            @pl.loop(0, PLANE)
            def _(n):
                to = q * PLANE + (place + n) % PLANE

                @pl.when(to != i)
                def _():
                    out_copy(h, to).start()

                @pl.when(to == i)
                def _():
                    pltpu.make_async_copy(ready.at[h, to], *out_slot(h, i)).start()

    wait_weights(0)
    start_parts(0)
    mean = got_square[c]
    for d in range(1, CHAN):
        source = (c + d) % CHAN
        send(got_square.at[c], got_square.at[source], s_send.at[d], s_recv.at[source], i, source).wait_recv()
        mean = mean + got_square[source]
    scale = lax.rsqrt(mean[0:1] * (1.0 / (CHAN * feats)) + EPS)
    for d in range(1, CHAN):
        plane_copy((c + d) % CHAN, c, d).wait_recv()
    finish_parts(0, scale)
    branches_of(0)
    wait_weights(1)
    start_parts(1)
    start_outputs(0)
    finish_parts(1, scale)
    branches_of(1)
    start_outputs(1)

    for h in range(2):

        @pl.loop(0, CTX)
        def _(source):
            pltpu.make_async_copy(ready.at[h, 0], *out_slot(h, source)).wait()

    for h in range(2):

        @pl.loop(1, CTX)
        def _(j):
            weight_copy(h, j).wait_send()
            out_copy(h, (i + j) % CTX).wait_send()

        part_copy(h, far, 0).wait_send()
        part_copy(h, far + 1, 1).wait_send()
        part_copy(h, other, 2).wait_send()

    @pl.when(plane != c)
    def _():
        weight_copy(0, 0).wait_send()
        weight_copy(1, 0).wait_send()
        token_copy(0).wait_send()

    @pl.loop(1, PLANE)
    def _(n):
        token_copy(n).wait_send()

    for d in range(1, CHAN):
        square_copy(d).wait_send()
        plane_copy(c, (c + d) % CHAN, d).wait_send()


def gathered(
    token_ids, embed_table, norm_gain, in_weight, short_filter, residue, decay_rate, skip_bias
):
    f32, bf16 = jnp.float32, jnp.bfloat16
    rows = token_ids.shape[0]
    vocab, feats = embed_table.shape
    chans = decay_rate.shape[1]
    weight = jnp.transpose(in_weight, (1, 0, 2))
    operands = (token_ids, embed_table, norm_gain, weight, short_filter, residue, decay_rate, skip_bias)
    dma, vmem = pltpu.SemaphoreType.DMA, pltpu.VMEM
    return pl.pallas_call(
        main_kernel,
        name="hyena",
        out_shape=jax.ShapeDtypeStruct((2, PER, CTX * OWN, HALF), bf16),
        in_specs=[pl.BlockSpec(memory_space=pl.ANY)] * len(operands),
        out_specs=pl.BlockSpec(memory_space=pl.ANY),
        scratch_shapes=[
            vmem(token_ids.shape, jnp.int32),
            vmem((1, rows), jnp.int32),
            vmem(embed_table.shape, bf16),
            vmem(norm_gain.shape, f32),
            vmem(weight.shape, bf16),
            vmem(short_filter.shape, f32),
            vmem(residue.shape, f32),
            vmem(decay_rate.shape, f32),
            vmem(skip_bias.shape, f32),
            vmem((CTX, 3 * OWN, in_weight.shape[0]), bf16),
            vmem((CHAN, 3 * OWN, feats), bf16),
            vmem((CHAN, 8, vocab), f32),
            vmem((vocab, feats), bf16),
            vmem((2, 3 * OWN, vocab), f32),
            vmem((CHAN, WEIGHT_ROWS[0][1], vocab), bf16),
            vmem((CHAN, WEIGHT_ROWS[1][1], vocab), bf16),
            vmem((CHAN, WEIGHT_ROWS[0][1], vocab), bf16),
            vmem((CHAN, WEIGHT_ROWS[1][1], vocab), bf16),
            vmem((CTX, 1, rows), jnp.int32),
            vmem((3 * OWN, vocab), f32),
            vmem((2, SEG, 2 * FEWS), bf16),
            vmem((2, FEW * SEG + 3 * FEWS, SEG), bf16),
            vmem((2, 3, 3 * FEW, HALF), f32),
            vmem((2, FEW, SEG), f32),
            vmem((2, SEGS * FEW, SEG), f32),
            vmem((2, SEGS * FEW, SEG), f32),
            vmem((2, SEGS, FEWS), f32),
            vmem((2, CTX, PER, 2 * FEW, HALF), bf16),
            dma((8,)),
            dma((2, CTX)), dma((2, CTX)), dma((PLANE,)), dma((PLANE,)),
            dma((CHAN,)), dma((CHAN,)), dma((CHAN,)), dma((CHAN,)), dma((2, CHAN)), dma((2, CHAN)),
            dma((2, CTX)), dma((2, CTX)),
        ],
        compiler_params=pltpu.CompilerParams(
            collective_id=0, has_side_effects=True, vmem_limit_bytes=VMEM_LIMIT
        ),
    )(*operands)


def turn_kernel(got_hbm, out_hbm, got, out, in_sem, out_sem):
    f32, bf16 = jnp.float32, jnp.bfloat16
    unit = (
        lax.broadcasted_iota(jnp.int32, (HALF, HALF), 0) == lax.broadcasted_iota(jnp.int32, (HALF, HALF), 1)
    ).astype(bf16)
    loads = [pltpu.make_async_copy(got_hbm.at[:, g], got.at[:, g], in_sem.at[g]) for g in range(PER)]
    stores = []
    for load in loads:
        load.start()
    for g in range(PER):
        loads[g].wait()
        eights = [got[h, g].astype(f32).reshape(CTX, 2, FEW, HALF) for h in range(2)]
        for half in range(2):
            rows = jnp.concatenate([eights[h][:, half : half + 1] for h in range(2)], axis=1)
            rows = rows.reshape(CTX * OWN, HALF).astype(bf16)
            top = g * SEG + half * HALF
            turned = lax.dot_general(unit, rows, NT, preferred_element_type=f32)
            out[top : top + HALF, :] = turned.astype(bf16)
        rows = pl.ds(g * SEG, SEG)
        stores.append(pltpu.make_async_copy(out.at[rows, :], out_hbm.at[rows, :], out_sem.at[g]))
        stores[g].start()
    for store in stores:
        store.wait()


def turned(got):
    bf16 = jnp.bfloat16
    shape = (PER * SEG, CTX * OWN)
    return pl.pallas_call(
        turn_kernel,
        name="turn",
        out_shape=jax.ShapeDtypeStruct(shape, bf16),
        in_specs=[pl.BlockSpec(memory_space=pl.ANY)],
        out_specs=pl.BlockSpec(memory_space=pl.ANY),
        scratch_shapes=[
            pltpu.VMEM(got.shape, bf16),
            pltpu.VMEM(shape, bf16),
            pltpu.SemaphoreType.DMA((PER,)),
            pltpu.SemaphoreType.DMA((PER,)),
        ],
        compiler_params=pltpu.CompilerParams(vmem_limit_bytes=VMEM_LIMIT),
    )(got)


def per_device(*arrays):
    return turned(gathered(*arrays))


def solution(mesh):
    return jax.shard_map(
        per_device,
        mesh=mesh,
        in_specs=(
            P("ctx"),
            P(None, "chan"),
            P(),
            P("ctx", None, "chan"),
            P(None, None, "chan"),
            P(None, "chan"),
            P(None, "chan"),
            P("chan"),
        ),
        out_specs=P("ctx", "chan"),
        check_vma=False,
    )
```

time: 57.9 us -> 47.9 us (0.83); the launches traced: 56.9 us -> 47.7 us
  local copies, waits for them, and re-layouts: 6.56 us -> 0 us
  Pallas kernels: 50.3 us -> 47.7 us
    unnamed x16 -> x0, local copies, waits for them, and re-layouts: 6.56 us -> none
    pallas_call x1, Pallas kernels: 49 us -> 45.3 us  [gathered(): pl.pallas_call(main_kernel, name='hyena', out_shape=jax.ShapeDtypeStruct(...]
    pallas_call x1, Pallas kernels: 1.28 us -> 2.41 us  [turned(): pl.pallas_call(turn_kernel, name='turn', out_shape=jax.ShapeDtypeStruct(s...]
where the time goes in v3:
time: 47.9 us; the launch traced here: 47.7 us
  Pallas kernels  47.7 us (100%)
    pallas_call x1, Pallas kernels, gathered(): pl.pallas_call(main_kernel, name='hyena', out_shape=jax.ShapeDtypeStruct(...  45.3 us
    pallas_call x1, Pallas kernels, turned(): pl.pallas_call(turn_kernel, name='turn', out_shape=jax.ShapeDtypeStruct(s...  2.41 us

profile of v3, /device:TPU:0, one launch (start us, length us, event | category | flops | bytes accessed | tf_op | source)
XLA Modules:
  0.0 47.7 jit_solution(2714519162980348371)
XLA Ops:
  0.0 45.3 %hyena.1.got_hbm = bf16[2,3,512,128]{3,2,1,0:T(8,128)(2,1)} custom-call(s32[768]{0:T(1024)} %tok_hbm.1, bf16[512,1024]{1,0:T(8,128)(2,1)} %embed_hbm.1, f32[4096]{0:T(1024)} %gain_hbm.1, bf16[3,128,512]{2,1,0:T(8,128)(2,1)} %bitcast.1, f32[3,3,512]{2,1,0:T(4,128)} %taps_hbm.1, f32[16,512]{1,0:T(8,128)} %residue_hbm.1, f32[16,512]{1,0:T(8,128)} %decay_hbm.1, ...), custom_call_target="tpu_custom_call" | custom-call | tf_op jit(solution)/shard_map/hyena/pallas_call | solution.py:461
  45.3 2.4 %turn.1 = bf16[768,512]{1,0:T(8,128)(2,1)} custom-call(bf16[2,3,512,128]{3,2,1,0:T(8,128)(2,1)} %hyena.1.got_hbm), custom_call_target="tpu_custom_call" | custom-call | tf_op jit(solution)/shard_map/turn/pallas_call | solution.py:535

commit v4 on v3

--- a/solution.py
+++ b/solution.py
@@ -234,12 +234,12 @@
     def weight_slices(h, to, slot):
         rows = pl.ds(*WEIGHT_ROWS[h])
         lanes = pl.ds(pl.multiple_of(slot % PLANE * HALF, HALF), HALF)
-        return turned_weight.at[to, rows, :], got_weight.at[slot // PLANE, rows, lanes], w_recv.at[h, slot]
+        return turned_weight.at[to, rows, :], got_weight.at[slot // PLANE, rows, lanes], w_recv.at[h]
 
     def weight_copy(h, j):
         to = (i + j) % CTX
         src, dst, sem = weight_slices(h, to, c * PLANE + place)
-        return send(src, dst, w_send.at[h, j], sem, to, plane)
+        return send(src, dst, w_send.at[h], sem, to, plane)
 
     def start_weights(h):
         @pl.loop(1, CTX)
@@ -254,16 +254,18 @@
         def _():
             weight_copy(h, 0).start()
 
+    def wait_for(region, sem):
+        pltpu.make_async_copy(region, region, sem).wait()
+
     def wait_weights(h):
-        @pl.loop(0, CTX)
-        def _(slot):
-            pltpu.make_async_copy(*weight_slices(h, 0, slot)).wait()
+        wait_for(got_weight.at[:, pl.ds(*WEIGHT_ROWS[h]), :], w_recv.at[h])
 
     def token_copy(n):
         to = c * PLANE + (place + n) % PLANE
-        return send(own_tokens, tokens.at[i], t_send.at[n], t_recv.at[place], to, plane)
-
-    own_token_copy = pltpu.make_async_copy(own_tokens, tokens.at[i], t_recv.at[place])
+        return send(own_tokens, tokens.at[i], t_send, t_recv, to, plane)
+
+    start_weights(0)
+    own_token_copy = pltpu.make_async_copy(own_tokens, tokens.at[i], t_recv)
 
     @pl.when(plane == c)
     def _():
@@ -277,7 +279,7 @@
     def _(n):
         token_copy(n).start()
 
-    start_weights(0)
+    start_weights(1)
 
     loads[2].wait()
     loads[3].wait()
@@ -295,9 +297,7 @@
         square_copy(d).start()
     scaled[...] = (wide * gain[pl.ds(c * feats, feats)].reshape(1, feats)).astype(bf16)
 
-    @pl.loop(0, PLANE)
-    def _(n):
-        pltpu.make_async_copy(own_tokens, tokens.at[c * PLANE + n], t_recv.at[n]).wait()
+    wait_for(tokens.at[pl.ds(c * PLANE, PLANE)], t_recv)
 
     def plane_copy(source, to, d):
         block = tokens.at[pl.ds(source * PLANE, PLANE)]
@@ -305,6 +305,77 @@
 
     for d in range(1, CHAN):
         plane_copy(c, (c + d) % CHAN, d).start()
+
+    near, far = (c // 2) * 2, 2 - (c // 2) * 2
+    other = c + 1 - 2 * (c % 2)
+    part_send, part_got = (part_send0, part_send1), (part_got0, part_got1)
+
+    def part_copy(h, to, d):
+        return send(part_send[h].at[to], part_got[h].at[c], p_send.at[h, d], p_recv.at[h, c], i, to)
+
+    def products(h, first):
+        top, count = WEIGHT_ROWS[h]
+        weights = got_weight[pl.ds(first, 2), pl.ds(top, count), :].reshape(2 * count, feats)
+        product = lax.dot_general(weights, scaled[...], NT, preferred_element_type=f32)
+        return product.reshape(2, count, product.shape[1])
+
+    def start_parts(h):
+        top, count = WEIGHT_ROWS[h]
+        part_send[h][pl.ds(far, 2)] = products(h, far).astype(bf16)
+        part_copy(h, far, 0).start()
+        part_copy(h, far + 1, 1).start()
+        product = products(h, near)
+        part[:, top : top + count, :] = product
+        part_send[h][pl.ds(near, 2)] = product.astype(bf16)
+        part_copy(h, other, 2).start()
+
+    def finish_parts(h, scale):
+        top, count = WEIGHT_ROWS[h]
+        total = part[c % 2, top : top + count, :]
+        for d in range(1, CHAN):
+            source = (c + d) % CHAN
+            send(
+                part_send[h].at[0], part_got[h].at[source], p_send.at[h, d], p_recv.at[h, source], i, source
+            ).wait_recv()
+            total = total + part_got[h][source].astype(f32)
+        table[top : top + count, :] = (total * scale).astype(bf16).astype(f32)
+
+    def branches_of(h):
+        rows = jnp.concatenate([table[top : top + FEW, :] for top in TABLE_ROWS[h]], axis=0)
+        halves = jnp.concatenate([rows[:, :SEG], rows[:, SEG:]], axis=0).astype(bf16)
+        short_filter_and_gate(halves, tokens, taps.at[h], carried.at[h], query.at[h])
+
+    def out_slot(h, source):
+        return got_ref.at[h, :, pl.ds(pl.multiple_of(source * OWN, OWN), OWN), :], o_recv.at[h]
+
+    def out_copy(h, to):
+        dst, sem = out_slot(h, i)
+        return send(ready.at[h, to], dst, o_send.at[h], sem, to, c)
+
+    def start_outputs(h, decay_row):
+        segment_states(carried.at[h], gather.at[h], decay_row[:, h * FEWS : (h + 1) * FEWS], state.at[h])
+
+        @pl.loop(0, CTX // PLANE)
+        def _(step):
+            q = (plane + 1 + step) % (CTX // PLANE)
+            outputs_of_part(
+                q, carried.at[h], query.at[h], state.at[h], reach.at[h], skip.at[h], ready.at[h]
+            )
+
+            @pl.loop(0, PLANE)
+            def _(n):
+                to = q * PLANE + (place + n) % PLANE
+
+                @pl.when(to != i)
+                def _():
+                    out_copy(h, to).start()
+
+                @pl.when(to == i)
+                def _():
+                    pltpu.make_async_copy(ready.at[h, to], *out_slot(h, i)).start()
+
+    wait_weights(0)
+    start_parts(0)
 
     for load in loads[4:]:
         load.wait()
@@ -327,78 +398,8 @@
     skip_column = jnp.transpose(skip_row)[:OWN, 0:1]
     skip[...] = jnp.broadcast_to(skip_column, (OWN, SEG)).reshape(2, FEW, SEG)
 
-    start_weights(1)
-
-    near, far = (c // 2) * 2, 2 - (c // 2) * 2
-    other = c + 1 - 2 * (c % 2)
-    part_send, part_got = (part_send0, part_send1), (part_got0, part_got1)
-
-    def part_copy(h, to, d):
-        return send(part_send[h].at[to], part_got[h].at[c], p_send.at[h, d], p_recv.at[h, c], i, to)
-
-    def products(h, first):
-        top, count = WEIGHT_ROWS[h]
-        weights = got_weight[pl.ds(first, 2), pl.ds(top, count), :].reshape(2 * count, feats)
-        product = lax.dot_general(weights, scaled[...], NT, preferred_element_type=f32)
-        return product.reshape(2, count, product.shape[1])
-
-    def start_parts(h):
-        top, count = WEIGHT_ROWS[h]
-        part_send[h][pl.ds(far, 2)] = products(h, far).astype(bf16)
-        part_copy(h, far, 0).start()
-        part_copy(h, far + 1, 1).start()
-        product = products(h, near)
-        part[:, top : top + count, :] = product
-        part_send[h][pl.ds(near, 2)] = product.astype(bf16)
-        part_copy(h, other, 2).start()
-
-    def finish_parts(h, scale):
-        top, count = WEIGHT_ROWS[h]
-        total = part[c % 2, top : top + count, :]
-        for d in range(1, CHAN):
-            source = (c + d) % CHAN
-            send(
-                part_send[h].at[0], part_got[h].at[source], p_send.at[h, d], p_recv.at[h, source], i, source
-            ).wait_recv()
-            total = total + part_got[h][source].astype(f32)
-        table[top : top + count, :] = (total * scale).astype(bf16).astype(f32)
-
-    def branches_of(h):
-        rows = jnp.concatenate([table[top : top + FEW, :] for top in TABLE_ROWS[h]], axis=0)
-        halves = jnp.concatenate([rows[:, :SEG], rows[:, SEG:]], axis=0).astype(bf16)
-        short_filter_and_gate(halves, tokens, taps.at[h], carried.at[h], query.at[h])
-
-    def out_slot(h, source):
-        return got_ref.at[h, :, pl.ds(pl.multiple_of(source * OWN, OWN), OWN), :], o_recv.at[h, source]
-
-    def out_copy(h, to):
-        dst, sem = out_slot(h, i)
-        return send(ready.at[h, to], dst, o_send.at[h, to], sem, to, c)
-
-    def start_outputs(h):
-        segment_states(carried.at[h], gather.at[h], decay_row[:, h * FEWS : (h + 1) * FEWS], state.at[h])
-
-        @pl.loop(0, CTX // PLANE)
-        def _(step):
-            q = (plane + 1 + step) % (CTX // PLANE)
-            outputs_of_part(
-                q, carried.at[h], query.at[h], state.at[h], reach.at[h], skip.at[h], ready.at[h]
-            )
-
-            @pl.loop(0, PLANE)
-            def _(n):
-                to = q * PLANE + (place + n) % PLANE
-
-                @pl.when(to != i)
-                def _():
-                    out_copy(h, to).start()
-
-                @pl.when(to == i)
-                def _():
-                    pltpu.make_async_copy(ready.at[h, to], *out_slot(h, i)).start()
-
-    wait_weights(0)
-    start_parts(0)
+    wait_weights(1)
+    start_parts(1)
     mean = got_square[c]
     for d in range(1, CHAN):
         source = (c + d) % CHAN
@@ -409,43 +410,36 @@
         plane_copy((c + d) % CHAN, c, d).wait_recv()
     finish_parts(0, scale)
     branches_of(0)
-    wait_weights(1)
-    start_parts(1)
-    start_outputs(0)
+    start_outputs(0, decay_row)
     finish_parts(1, scale)
     branches_of(1)
-    start_outputs(1)
+    start_outputs(1, decay_row)
 
     for h in range(2):
-
-        @pl.loop(0, CTX)
-        def _(source):
-            pltpu.make_async_copy(ready.at[h, 0], *out_slot(h, source)).wait()
-
-    for h in range(2):
-
-        @pl.loop(1, CTX)
-        def _(j):
-            weight_copy(h, j).wait_send()
-            out_copy(h, (i + j) % CTX).wait_send()
-
+        wait_for(ready.at[h, pl.ds(0, CTX - 1)], o_send.at[h])
         part_copy(h, far, 0).wait_send()
         part_copy(h, far + 1, 1).wait_send()
         part_copy(h, other, 2).wait_send()
 
+    def wait_sends(skipped):
+        for h in range(2):
+            rows = pl.ds(*WEIGHT_ROWS[h])
+            wait_for(turned_weight.at[pl.ds(0, CTX - skipped), rows, :], w_send.at[h])
+        wait_for(tokens.at[pl.ds(0, PLANE - skipped)], t_send)
+
     @pl.when(plane != c)
     def _():
-        weight_copy(0, 0).wait_send()
-        weight_copy(1, 0).wait_send()
-        token_copy(0).wait_send()
-
-    @pl.loop(1, PLANE)
-    def _(n):
-        token_copy(n).wait_send()
+        wait_sends(0)
+
+    @pl.when(plane == c)
+    def _():
+        wait_sends(1)
 
     for d in range(1, CHAN):
         square_copy(d).wait_send()
         plane_copy(c, (c + d) % CHAN, d).wait_send()
+    for h in range(2):
+        wait_for(got_ref.at[h], o_recv.at[h])
 
 
 def gathered(
@@ -494,9 +488,9 @@
             vmem((2, SEGS, FEWS), f32),
             vmem((2, CTX, PER, 2 * FEW, HALF), bf16),
             dma((8,)),
-            dma((2, CTX)), dma((2, CTX)), dma((PLANE,)), dma((PLANE,)),
+            dma((2,)), dma((2,)), dma(()), dma(()),
             dma((CHAN,)), dma((CHAN,)), dma((CHAN,)), dma((CHAN,)), dma((2, CHAN)), dma((2, CHAN)),
-            dma((2, CTX)), dma((2, CTX)),
+            dma((2,)), dma((2,)),
         ],
         compiler_params=pltpu.CompilerParams(
             collective_id=0, has_side_effects=True, vmem_limit_bytes=VMEM_LIMIT

time: 47.9 us -> 45.8 us (0.956)
  Pallas kernels: 47.7 us -> 45.7 us
    pallas_call x1, Pallas kernels: 45.3 us -> 43.2 us  [gathered(): pl.pallas_call(main_kernel, name='hyena', out_shape=jax.ShapeDtypeStruct(...]
where the time goes in v4:
time: 45.8 us; the launch traced here: 45.7 us
  Pallas kernels  45.7 us (100%)
    pallas_call x1, Pallas kernels, gathered(): pl.pallas_call(main_kernel, name='hyena', out_shape=jax.ShapeDtypeStruct(...  43.2 us
    pallas_call x1, Pallas kernels, turned(): pl.pallas_call(turn_kernel, name='turn', out_shape=jax.ShapeDtypeStruct(s...  2.41 us

profile of v4, /device:TPU:0, one launch (start us, length us, event | category | flops | bytes accessed | tf_op | source)
XLA Modules:
  0.0 45.7 jit_solution(13650670395442313104)
XLA Ops:
  0.0 43.2 %hyena.1.got_hbm = bf16[2,3,512,128]{3,2,1,0:T(8,128)(2,1)} custom-call(s32[768]{0:T(1024)} %tok_hbm.1, bf16[512,1024]{1,0:T(8,128)(2,1)} %embed_hbm.1, f32[4096]{0:T(1024)} %gain_hbm.1, bf16[3,128,512]{2,1,0:T(8,128)(2,1)} %bitcast.1, f32[3,3,512]{2,1,0:T(4,128)} %taps_hbm.1, f32[16,512]{1,0:T(8,128)} %residue_hbm.1, f32[16,512]{1,0:T(8,128)} %decay_hbm.1, ...), custom_call_target="tpu_custom_call" | custom-call | tf_op jit(solution)/shard_map/hyena/pallas_call | solution.py:455
  43.3 2.4 %turn.1 = bf16[768,512]{1,0:T(8,128)(2,1)} custom-call(bf16[2,3,512,128]{3,2,1,0:T(8,128)(2,1)} %hyena.1.got_hbm), custom_call_target="tpu_custom_call" | custom-call | tf_op jit(solution)/shard_map/turn/pallas_call | solution.py:529

commit v5 on v4

--- a/solution.py
+++ b/solution.py
@@ -9,7 +9,8 @@
 
 MESH = pl.DeviceIdType.MESH
 EPS = 1e-06
-VMEM_LIMIT = 60 * 1024 * 1024
+VMEM_LIMIT = 56 * 1024 * 1024
+TURN_LIMIT = 16 * 1024 * 1024
 
 CTX, CHAN, PLANE = 32, 4, 8
 OWN = 16
@@ -264,7 +265,6 @@
         to = c * PLANE + (place + n) % PLANE
         return send(own_tokens, tokens.at[i], t_send, t_recv, to, plane)
 
-    start_weights(0)
     own_token_copy = pltpu.make_async_copy(own_tokens, tokens.at[i], t_recv)
 
     @pl.when(plane == c)
@@ -279,7 +279,7 @@
     def _(n):
         token_copy(n).start()
 
-    start_weights(1)
+    start_weights(0)
 
     loads[2].wait()
     loads[3].wait()
@@ -290,6 +290,15 @@
     squares = lax.dot_general(ones, square_high, NT, preferred_element_type=f32)
     got_square[c] = squares + lax.dot_general(ones, square_low, NT, preferred_element_type=f32)
 
+    wait_for(tokens.at[pl.ds(c * PLANE, PLANE)], t_recv)
+
+    def plane_copy(source, to, d):
+        block = tokens.at[pl.ds(source * PLANE, PLANE)]
+        return send(block, block, u_send.at[d], u_recv.at[source], i, to)
+
+    for d in range(1, CHAN):
+        plane_copy(c, (c + d) % CHAN, d).start()
+
     def square_copy(d):
         return send(got_square.at[c], got_square.at[c], s_send.at[d], s_recv.at[c], i, (c + d) % CHAN)
 
@@ -297,15 +306,7 @@
         square_copy(d).start()
     scaled[...] = (wide * gain[pl.ds(c * feats, feats)].reshape(1, feats)).astype(bf16)
 
-    wait_for(tokens.at[pl.ds(c * PLANE, PLANE)], t_recv)
-
-    def plane_copy(source, to, d):
-        block = tokens.at[pl.ds(source * PLANE, PLANE)]
-        return send(block, block, u_send.at[d], u_recv.at[source], i, to)
-
-    for d in range(1, CHAN):
-        plane_copy(c, (c + d) % CHAN, d).start()
-
+    start_weights(1)
     near, far = (c // 2) * 2, 2 - (c // 2) * 2
     other = c + 1 - 2 * (c % 2)
     part_send, part_got = (part_send0, part_send1), (part_got0, part_got1)
@@ -455,7 +456,7 @@
     return pl.pallas_call(
         main_kernel,
         name="hyena",
-        out_shape=jax.ShapeDtypeStruct((2, PER, CTX * OWN, HALF), bf16),
+        out_shape=pltpu.VMEM((2, PER, CTX * OWN, HALF), bf16),
         in_specs=[pl.BlockSpec(memory_space=pl.ANY)] * len(operands),
         out_specs=pl.BlockSpec(memory_space=pl.ANY),
         scratch_shapes=[
@@ -498,17 +499,13 @@
     )(*operands)
 
 
-def turn_kernel(got_hbm, out_hbm, got, out, in_sem, out_sem):
+def turn_kernel(got, out_hbm, out, out_sem):
     f32, bf16 = jnp.float32, jnp.bfloat16
     unit = (
         lax.broadcasted_iota(jnp.int32, (HALF, HALF), 0) == lax.broadcasted_iota(jnp.int32, (HALF, HALF), 1)
     ).astype(bf16)
-    loads = [pltpu.make_async_copy(got_hbm.at[:, g], got.at[:, g], in_sem.at[g]) for g in range(PER)]
     stores = []
-    for load in loads:
-        load.start()
     for g in range(PER):
-        loads[g].wait()
         eights = [got[h, g].astype(f32).reshape(CTX, 2, FEW, HALF) for h in range(2)]
         for half in range(2):
             rows = jnp.concatenate([eights[h][:, half : half + 1] for h in range(2)], axis=1)
@@ -530,15 +527,10 @@
         turn_kernel,
         name="turn",
         out_shape=jax.ShapeDtypeStruct(shape, bf16),
-        in_specs=[pl.BlockSpec(memory_space=pl.ANY)],
+        in_specs=[pl.BlockSpec(memory_space=pltpu.VMEM)],
         out_specs=pl.BlockSpec(memory_space=pl.ANY),
-        scratch_shapes=[
-            pltpu.VMEM(got.shape, bf16),
-            pltpu.VMEM(shape, bf16),
-            pltpu.SemaphoreType.DMA((PER,)),
-            pltpu.SemaphoreType.DMA((PER,)),
-        ],
-        compiler_params=pltpu.CompilerParams(vmem_limit_bytes=VMEM_LIMIT),
+        scratch_shapes=[pltpu.VMEM(shape, bf16), pltpu.SemaphoreType.DMA((PER,))],
+        compiler_params=pltpu.CompilerParams(vmem_limit_bytes=TURN_LIMIT),
     )(got)
 
 

time: 45.8 us -> 42.2 us (0.921)
  Pallas kernels: 45.7 us -> 41.8 us
    pallas_call x1, Pallas kernels: 43.2 us -> 40.7 us  [gathered(): pl.pallas_call(main_kernel, name='hyena', out_shape=pltpu.VMEM((2, PER, C...]
    pallas_call x1, Pallas kernels: 2.41 us -> 1.14 us  [turned(): pl.pallas_call(turn_kernel, name='turn', out_shape=jax.ShapeDtypeStruct(s...]
where the time goes in v5:
time: 42.2 us; the launch traced here: 41.8 us
  Pallas kernels  41.8 us (99%)
    pallas_call x1, Pallas kernels, gathered(): pl.pallas_call(main_kernel, name='hyena', out_shape=pltpu.VMEM((2, PER, C...  40.7 us
    pallas_call x1, Pallas kernels, turned(): pl.pallas_call(turn_kernel, name='turn', out_shape=jax.ShapeDtypeStruct(s...  1.14 us

profile of v5, /device:TPU:0, one launch (start us, length us, event | category | flops | bytes accessed | tf_op | source)
XLA Modules:
  0.0 41.8 jit_solution(14242473286546853319)
XLA Ops:
  0.0 40.7 %hyena.1.got = bf16[2,3,512,128]{3,2,1,0:T(8,128)(2,1)S(1)} custom-call(s32[768]{0:T(1024)} %tok_hbm.1, bf16[512,1024]{1,0:T(8,128)(2,1)} %embed_hbm.1, f32[4096]{0:T(1024)} %gain_hbm.1, bf16[3,128,512]{2,1,0:T(8,128)(2,1)} %bitcast.1, f32[3,3,512]{2,1,0:T(4,128)} %taps_hbm.1, f32[16,512]{1,0:T(8,128)} %residue_hbm.1, f32[16,512]{1,0:T(8,128)} %decay_hbm.1, ...), custom_call_target="tpu_custom_call" | custom-call | tf_op jit(solution)/shard_map/hyena/pallas_call | solution.py:456
  40.7 1.1 %turn.1 = bf16[768,512]{1,0:T(8,128)(2,1)} custom-call(bf16[2,3,512,128]{3,2,1,0:T(8,128)(2,1)S(1)} %hyena.1.got), custom_call_target="tpu_custom_call" | custom-call | tf_op jit(solution)/shard_map/turn/pallas_call | solution.py:526

commit v6 on v5

--- a/solution.py
+++ b/solution.py
@@ -113,16 +113,17 @@
 def short_filter_and_gate(table, tokens_ref, taps_ref, carried_ref, query_ref):
     f32, bf16 = jnp.float32, jnp.bfloat16
     rows = 3 * FEW
-    entry = lax.broadcasted_iota(jnp.int32, (SEG, SEG), 0).astype(f32).astype(bf16)
+    entry = lax.broadcasted_iota(jnp.int32, (HALF, SEG), 0).astype(f32).astype(bf16)
     lane = lax.broadcasted_iota(jnp.int32, (rows, HALF), 1)
     one, zero = jnp.ones((), bf16), jnp.zeros((), bf16)
 
     def block(g, before):
         for part in range(PER):
             ids = tokens_ref[g, :, part * SEG : (part + 1) * SEG]
-            chosen = (ids & (SEG - 1)).astype(f32).astype(bf16)
-            both = dot(table, jnp.where(entry == chosen, one, zero))
-            projected = jnp.where(ids >= SEG, both[rows:], both[:rows])
+            chosen = (ids & (HALF - 1)).astype(f32).astype(bf16)
+            each = dot(table, jnp.where(entry == chosen, one, zero)).reshape(4, rows, SEG)
+            odd, upper = (ids & HALF) != 0, (ids & SEG) != 0
+            projected = jnp.where(upper, jnp.where(odd, each[3], each[2]), jnp.where(odd, each[1], each[0]))
             at = pl.ds(pl.multiple_of((g * PER + part) * FEW, FEW), FEW)
             for half in range(2):
                 lanes = slice(half * HALF, (half + 1) * HALF)
@@ -343,8 +344,8 @@
 
     def branches_of(h):
         rows = jnp.concatenate([table[top : top + FEW, :] for top in TABLE_ROWS[h]], axis=0)
-        halves = jnp.concatenate([rows[:, :SEG], rows[:, SEG:]], axis=0).astype(bf16)
-        short_filter_and_gate(halves, tokens, taps.at[h], carried.at[h], query.at[h])
+        quarters = jnp.concatenate([rows[:, n * HALF : (n + 1) * HALF] for n in range(4)], axis=0)
+        short_filter_and_gate(quarters.astype(bf16), tokens, taps.at[h], carried.at[h], query.at[h])
 
     def out_slot(h, source):
         return got_ref.at[h, :, pl.ds(pl.multiple_of(source * OWN, OWN), OWN), :], o_recv.at[h]

time: 42.2 us -> 41.1 us (0.974)
  Pallas kernels: 41.8 us -> 40.7 us
    pallas_call x1, Pallas kernels: 40.7 us -> 39.6 us  [gathered(): pl.pallas_call(main_kernel, name='hyena', out_shape=pltpu.VMEM((2, PER, C...]
where the time goes in v6:
time: 41.1 us; the launch traced here: 40.7 us
  Pallas kernels  40.7 us (99%)
    pallas_call x1, Pallas kernels, gathered(): pl.pallas_call(main_kernel, name='hyena', out_shape=pltpu.VMEM((2, PER, C...  39.6 us
    pallas_call x1, Pallas kernels, turned(): pl.pallas_call(turn_kernel, name='turn', out_shape=jax.ShapeDtypeStruct(s...  1.15 us

profile of v6, /device:TPU:0, one launch (start us, length us, event | category | flops | bytes accessed | tf_op | source)
XLA Modules:
  0.0 40.7 jit_solution(10305547096291115869)
XLA Ops:
  0.0 39.6 %hyena.1.got = bf16[2,3,512,128]{3,2,1,0:T(8,128)(2,1)S(1)} custom-call(s32[768]{0:T(1024)} %tok_hbm.1, bf16[512,1024]{1,0:T(8,128)(2,1)} %embed_hbm.1, f32[4096]{0:T(1024)} %gain_hbm.1, bf16[3,128,512]{2,1,0:T(8,128)(2,1)} %bitcast.1, f32[3,3,512]{2,1,0:T(4,128)} %taps_hbm.1, f32[16,512]{1,0:T(8,128)} %residue_hbm.1, f32[16,512]{1,0:T(8,128)} %decay_hbm.1, ...), custom_call_target="tpu_custom_call" | custom-call | tf_op jit(solution)/shard_map/hyena/pallas_call | solution.py:457
  39.6 1.1 %turn.1 = bf16[768,512]{1,0:T(8,128)(2,1)} custom-call(bf16[2,3,512,128]{3,2,1,0:T(8,128)(2,1)S(1)} %hyena.1.got), custom_call_target="tpu_custom_call" | custom-call | tf_op jit(solution)/shard_map/turn/pallas_call | solution.py:527

commit v7 on v6

--- a/solution.py
+++ b/solution.py
@@ -136,8 +136,8 @@
                 )
                 before = turned
                 carried = branches[FEW : 2 * FEW] * branches[2 * FEW :]
-                carried_ref[at, lanes] = carried.astype(bf16).astype(f32)
-                query_ref[at, lanes] = branches[:FEW]
+                carried_ref[half, at, :] = carried.astype(bf16).astype(f32)
+                query_ref[half, at, :] = branches[:FEW]
         return before
 
     nothing = jnp.zeros((rows, HALF), f32)
@@ -145,6 +145,10 @@
 
 
 UNROLL = 16
+
+
+def both_halves(ref, rows):
+    return jnp.concatenate([ref[half, rows, :] for half in range(2)], axis=1)
 
 
 def own_pairs():
@@ -154,7 +158,7 @@
 
 def segment_states(carried_ref, gather, decay_row, state_ref):
     f32, bf16 = jnp.float32, jnp.bfloat16
-    enters = dot(carried_ref[...].astype(bf16), gather[...])
+    enters = dot(both_halves(carried_ref, slice(None)).astype(bf16), gather[...])
     enters = (enters[:, :FEWS] + enters[:, FEWS:]).reshape(SEGS, FEW, FEWS)
     added = jnp.sum(jnp.where(own_pairs(), enters, 0.0), axis=1)
 
@@ -169,29 +173,36 @@
     state_ref[...] = state
 
 
-def outputs_of_part(q, carried_ref, query_ref, state_ref, reach, skip_ref, ready):
-    f32, bf16 = jnp.float32, jnp.bfloat16
+def inside_segments(carried_ref, reach, conv_ref):
+    for ch in range(FEW):
+        rows = pl.ds(ch, SEGS, stride=FEW)
+        conv = dot(both_halves(carried_ref, rows).astype(jnp.bfloat16), reach[ch * SEG : (ch + 1) * SEG, :])
+        for half in range(2):
+            conv_ref[half, rows, :] = conv[:, half * HALF : (half + 1) * HALF]
+
+
+def outputs_of_part(q, carried_ref, query_ref, state_ref, conv_ref, reach, skip_ref, ready):
     first = pl.multiple_of(q * PART, PART)
     rows = pl.ds(pl.multiple_of(first * FEW, FEW), PART * FEW)
-    carried = carried_ref[rows, :].reshape(PART, FEW, SEG)
-    channel = lax.broadcasted_iota(jnp.int32, (1, FEW, SEG), 1)
-    parts = [
-        jnp.where(channel == ch, carried, 0.0).reshape(PART * FEW, SEG).astype(bf16) for ch in range(FEW)
-    ]
     state = jnp.where(own_pairs(), state_ref[pl.ds(first, PART), :][:, None, :], 0.0)
     high, low = high_low(state.reshape(PART * FEW, FEWS))
-    conv = dot(jnp.concatenate(parts + [high, low, high], axis=1), reach[...])
-    gated = query_ref[rows, :] * (conv + (skip_ref[...][None] * carried).reshape(PART * FEW, SEG))
-    halves = [gated[:, half * HALF : (half + 1) * HALF].reshape(PART, 1, FEW, HALF) for half in range(2)]
+    reached = dot(jnp.concatenate([high, low, high], axis=1), reach[FEW * SEG :, :])
+    halves = []
+    for half in range(2):
+        lanes = slice(half * HALF, (half + 1) * HALF)
+        carried = carried_ref[half, rows, :].reshape(PART, FEW, HALF)
+        direct = (skip_ref[:, lanes][None] * carried).reshape(PART * FEW, HALF)
+        gated = query_ref[half, rows, :] * (conv_ref[half, rows, :] + reached[:, lanes] + direct)
+        halves.append(gated.reshape(PART, 1, FEW, HALF))
     block = jnp.concatenate(halves, axis=1).reshape(PLANE, PER, 2 * FEW, HALF)
-    ready[pl.ds(q * PLANE, PLANE)] = block.astype(bf16)
+    ready[pl.ds(q * PLANE, PLANE)] = block.astype(jnp.bfloat16)
 
 
 def main_kernel(
     tok_hbm, embed_hbm, gain_hbm, weight_hbm, taps_hbm, residue_hbm, decay_hbm, skip_hbm, got_ref,
     tok, own_tokens, embed, gain, weight, taps_all, residue, decay, skip_all,
     turned_weight, got_weight, got_square, scaled, part, part_send0, part_send1, part_got0, part_got1, tokens, table,
-    gather, reach, taps, skip, carried, query, state, ready,
+    gather, reach, taps, skip, carried, query, state, conv, ready,
     in_sem, w_send, w_recv, t_send, t_recv, u_send, u_recv, s_send, s_recv, p_send, p_recv, o_send, o_recv,
 ):
     f32, bf16 = jnp.float32, jnp.bfloat16
@@ -357,11 +368,13 @@
     def start_outputs(h, decay_row):
         segment_states(carried.at[h], gather.at[h], decay_row[:, h * FEWS : (h + 1) * FEWS], state.at[h])
 
+        inside_segments(carried.at[h], reach.at[h], conv)
+
         @pl.loop(0, CTX // PLANE)
         def _(step):
             q = (plane + 1 + step) % (CTX // PLANE)
             outputs_of_part(
-                q, carried.at[h], query.at[h], state.at[h], reach.at[h], skip.at[h], ready.at[h]
+                q, carried.at[h], query.at[h], state.at[h], conv, reach.at[h], skip.at[h], ready.at[h]
             )
 
             @pl.loop(0, PLANE)
@@ -485,9 +498,10 @@
             vmem((2, FEW * SEG + 3 * FEWS, SEG), bf16),
             vmem((2, 3, 3 * FEW, HALF), f32),
             vmem((2, FEW, SEG), f32),
-            vmem((2, SEGS * FEW, SEG), f32),
-            vmem((2, SEGS * FEW, SEG), f32),
+            vmem((2, 2, SEGS * FEW, HALF), f32),
+            vmem((2, 2, SEGS * FEW, HALF), f32),
             vmem((2, SEGS, FEWS), f32),
+            vmem((2, SEGS * FEW, HALF), f32),
             vmem((2, CTX, PER, 2 * FEW, HALF), bf16),
             dma((8,)),
             dma((2,)), dma((2,)), dma(()), dma(()),

time: 41.1 us -> 40.3 us (0.981)
  Pallas kernels: 40.7 us -> 40 us
    pallas_call x1, Pallas kernels: 39.6 us -> 38.8 us  [gathered(): pl.pallas_call(main_kernel, name='hyena', out_shape=pltpu.VMEM((2, PER, C...]
where the time goes in v7:
time: 40.3 us; the launch traced here: 40 us
  Pallas kernels  40 us (99%)
    pallas_call x1, Pallas kernels, gathered(): pl.pallas_call(main_kernel, name='hyena', out_shape=pltpu.VMEM((2, PER, C...  38.8 us
    pallas_call x1, Pallas kernels, turned(): pl.pallas_call(turn_kernel, name='turn', out_shape=jax.ShapeDtypeStruct(s...  1.15 us

profile of v7, /device:TPU:0, one launch (start us, length us, event | category | flops | bytes accessed | tf_op | source)
XLA Modules:
  0.0 40.0 jit_solution(1123411185169063617)
XLA Ops:
  0.0 38.8 %hyena.1.got = bf16[2,3,512,128]{3,2,1,0:T(8,128)(2,1)S(1)} custom-call(s32[768]{0:T(1024)} %tok_hbm.1, bf16[512,1024]{1,0:T(8,128)(2,1)} %embed_hbm.1, f32[4096]{0:T(1024)} %gain_hbm.1, bf16[3,128,512]{2,1,0:T(8,128)(2,1)} %bitcast.1, f32[3,3,512]{2,1,0:T(4,128)} %taps_hbm.1, f32[16,512]{1,0:T(8,128)} %residue_hbm.1, f32[16,512]{1,0:T(8,128)} %decay_hbm.1, ...), custom_call_target="tpu_custom_call" | custom-call | tf_op jit(solution)/shard_map/hyena/pallas_call | solution.py:470
  38.8 1.1 %turn.1 = bf16[768,512]{1,0:T(8,128)(2,1)} custom-call(bf16[2,3,512,128]{3,2,1,0:T(8,128)(2,1)S(1)} %hyena.1.got), custom_call_target="tpu_custom_call" | custom-call | tf_op jit(solution)/shard_map/turn/pallas_call | solution.py:541

commit v8 on v7

--- a/solution.py
+++ b/solution.py
@@ -250,7 +250,7 @@
         return turned_weight.at[to, rows, :], got_weight.at[slot // PLANE, rows, lanes], w_recv.at[h]
 
     def weight_copy(h, j):
-        to = (i + j) % CTX
+        to = (i + CTX - j) % CTX
         src, dst, sem = weight_slices(h, to, c * PLANE + place)
         return send(src, dst, w_send.at[h], sem, to, plane)
 

time: 40.3 us -> 39.8 us (0.988)
  Pallas kernels: 40 us -> 39.4 us
    pallas_call x1, Pallas kernels: 38.8 us -> 38.2 us  [gathered(): pl.pallas_call(main_kernel, name='hyena', out_shape=pltpu.VMEM((2, PER, C...]
where the time goes in v8:
time: 39.8 us; the launch traced here: 39.4 us
  Pallas kernels  39.4 us (99%)
    pallas_call x1, Pallas kernels, gathered(): pl.pallas_call(main_kernel, name='hyena', out_shape=pltpu.VMEM((2, PER, C...  38.2 us
    pallas_call x1, Pallas kernels, turned(): pl.pallas_call(turn_kernel, name='turn', out_shape=jax.ShapeDtypeStruct(s...  1.15 us

profile of v8, /device:TPU:0, one launch (start us, length us, event | category | flops | bytes accessed | tf_op | source)
XLA Modules:
  0.0 39.4 jit_solution(4676537111094732891)
XLA Ops:
  0.0 38.2 %hyena.1.got = bf16[2,3,512,128]{3,2,1,0:T(8,128)(2,1)S(1)} custom-call(s32[768]{0:T(1024)} %tok_hbm.1, bf16[512,1024]{1,0:T(8,128)(2,1)} %embed_hbm.1, f32[4096]{0:T(1024)} %gain_hbm.1, bf16[3,128,512]{2,1,0:T(8,128)(2,1)} %bitcast.1, f32[3,3,512]{2,1,0:T(4,128)} %taps_hbm.1, f32[16,512]{1,0:T(8,128)} %residue_hbm.1, f32[16,512]{1,0:T(8,128)} %decay_hbm.1, ...), custom_call_target="tpu_custom_call" | custom-call | tf_op jit(solution)/shard_map/hyena/pallas_call | solution.py:470
  38.2 1.1 %turn.1 = bf16[768,512]{1,0:T(8,128)(2,1)} custom-call(bf16[2,3,512,128]{3,2,1,0:T(8,128)(2,1)S(1)} %hyena.1.got), custom_call_target="tpu_custom_call" | custom-call | tf_op jit(solution)/shard_map/turn/pallas_call | solution.py:541

commit v9 on v8

--- a/solution.py
+++ b/solution.py
@@ -372,7 +372,7 @@
 
         @pl.loop(0, CTX // PLANE)
         def _(step):
-            q = (plane + 1 + step) % (CTX // PLANE)
+            q = (plane + (1 + step if h == 0 else CTX // PLANE - 1 - step)) % (CTX // PLANE)
             outputs_of_part(
                 q, carried.at[h], query.at[h], state.at[h], conv, reach.at[h], skip.at[h], ready.at[h]
             )

time: 39.8 us -> 39.8 us (level)
  no operation moved by 1% of the time
where the time goes in v9:
time: 39.8 us; the launch traced here: 39.5 us
  Pallas kernels  39.5 us (99%)
    pallas_call x1, Pallas kernels, gathered(): pl.pallas_call(main_kernel, name='hyena', out_shape=pltpu.VMEM((2, PER, C...  38.4 us
    pallas_call x1, Pallas kernels, turned(): pl.pallas_call(turn_kernel, name='turn', out_shape=jax.ShapeDtypeStruct(s...  1.15 us

profile of v9, /device:TPU:0, one launch (start us, length us, event | category | flops | bytes accessed | tf_op | source)
XLA Modules:
  0.0 39.5 jit_solution(16970982137811585465)
XLA Ops:
  0.0 38.4 %hyena.1.got = bf16[2,3,512,128]{3,2,1,0:T(8,128)(2,1)S(1)} custom-call(s32[768]{0:T(1024)} %tok_hbm.1, bf16[512,1024]{1,0:T(8,128)(2,1)} %embed_hbm.1, f32[4096]{0:T(1024)} %gain_hbm.1, bf16[3,128,512]{2,1,0:T(8,128)(2,1)} %bitcast.1, f32[3,3,512]{2,1,0:T(4,128)} %taps_hbm.1, f32[16,512]{1,0:T(8,128)} %residue_hbm.1, f32[16,512]{1,0:T(8,128)} %decay_hbm.1, ...), custom_call_target="tpu_custom_call" | custom-call | tf_op jit(solution)/shard_map/hyena/pallas_call | solution.py:470
  38.4 1.1 %turn.1 = bf16[768,512]{1,0:T(8,128)(2,1)} custom-call(bf16[2,3,512,128]{3,2,1,0:T(8,128)(2,1)S(1)} %hyena.1.got), custom_call_target="tpu_custom_call" | custom-call | tf_op jit(solution)/shard_map/turn/pallas_call | solution.py:541

commit v10 on v9

--- a/solution.py
+++ b/solution.py
@@ -144,7 +144,7 @@
     lax.fori_loop(0, SEGS // PER, block, (nothing, nothing), unroll=UNROLL)
 
 
-UNROLL = 16
+UNROLL = 32
 
 
 def both_halves(ref, rows):

time: 39.8 us -> 39.6 us (level)
  no operation moved by 1% of the time
where the time goes in v10:
time: 39.6 us; the launch traced here: 39.3 us
  Pallas kernels  39.2 us (99%)
    pallas_call x1, Pallas kernels, gathered(): pl.pallas_call(main_kernel, name='hyena', out_shape=pltpu.VMEM((2, PER, C...  38.1 us
    pallas_call x1, Pallas kernels, turned(): pl.pallas_call(turn_kernel, name='turn', out_shape=jax.ShapeDtypeStruct(s...  1.15 us

profile of v10, /device:TPU:0, one launch (start us, length us, event | category | flops | bytes accessed | tf_op | source)
XLA Modules:
  0.0 39.3 jit_solution(6409202729305211973)
XLA Ops:
  0.0 38.1 %hyena.1.got = bf16[2,3,512,128]{3,2,1,0:T(8,128)(2,1)S(1)} custom-call(s32[768]{0:T(1024)} %tok_hbm.1, bf16[512,1024]{1,0:T(8,128)(2,1)} %embed_hbm.1, f32[4096]{0:T(1024)} %gain_hbm.1, bf16[3,128,512]{2,1,0:T(8,128)(2,1)} %bitcast.1, f32[3,3,512]{2,1,0:T(4,128)} %taps_hbm.1, f32[16,512]{1,0:T(8,128)} %residue_hbm.1, f32[16,512]{1,0:T(8,128)} %decay_hbm.1, ...), custom_call_target="tpu_custom_call" | custom-call | tf_op jit(solution)/shard_map/hyena/pallas_call | solution.py:470
  38.1 1.1 %turn.1 = bf16[768,512]{1,0:T(8,128)(2,1)} custom-call(bf16[2,3,512,128]{3,2,1,0:T(8,128)(2,1)S(1)} %hyena.1.got), custom_call_target="tpu_custom_call" | custom-call | tf_op jit(solution)/shard_map/turn/pallas_call | solution.py:541
